TPU v7x, 32 devices: a whole 2x2x4 slice. The times are simulated.
32 devices in a mesh: blk: 8 (over z, y), circ: 4 (over x, core).
Axes of the slice: x: 2, y: 2, z: 4, core: 2. Of those that a mesh axis runs over, the one named last changes fastest.
Arguments:
- panels: float32 [4, 1024], P(None, ('blk', 'circ')), may hold values from -2 to 2, as said below
- node_of_panel: int32 [1024], P(('blk', 'circ')), may hold values from 0 to 2047, as said below
- stiffener_rows: int32 [4], replicated, may hold values from 0 to 63
- density_start: float32 [16, 1024], P(None, ('blk', 'circ')), may hold values from -6 to 6
- motion_start: float32 [16, 64, 1024], P(None, 'blk', 'circ'), may hold values from -6 to 6
- force: float32 [16, 64, 1024], P(None, 'blk', 'circ'), may hold values from -128 to 128
- stiffness: float32 [64, 1024], P('blk', 'circ'), may hold values from 0.5 to 2
Outputs:
- source_density: float32 [16, 1024], P(None, ('blk', 'circ'))
- surface_pressure: float32 [16, 1024], P(None, ('blk', 'circ'))
- shell_motion: float32 [16, 64, 1024], P(None, 'blk', 'circ')
Inputs may be any that keep to these rules, and one draw needn't show every extreme that they name: `panels`: every panel lies between 0.98 and 1.02 from the z axis, with z between -2 and 2 and area between 0.5 and 2 times 8 pi / 1024. `node_of_panel`: counted as row * 256 + column within the tile of the device that holds the panel. `stiffener_rows`: A row may be listed more than once.
All inputs are finite; a program needn't handle non-finite values.
Results may differ from a plain program's by a relative error of at most 0.0029.
Values may be sent and summed in bfloat16 or wider, within the bound.
A program may use at most 64 MiB of HBM per device.

v0:
```python
import math

import jax
import jax.numpy as jnp
from jax import lax
from jax.sharding import PartitionSpec as P

ITERS = 4
SWEEPS = 2


wave_number = 4.0
single_scale = 30.0
double_scale = 6.0
hoop_spring = 40.0
inertia_term = 4.0
loss_factor = 0.2
relaxation = 0.3


def padded(block, sides, width):
    for axis, dim in sides:
        count = lax.axis_size(axis)
        forward = [(i, i + 1) for i in range(count - 1)]
        forward.append((count - 1, 0))
        backward = [(target, source) for source, target in forward]
        low = lax.ppermute(
            lax.slice_in_dim(block, block.shape[dim] - width, None, axis=dim), axis, forward
        )
        high = lax.ppermute(lax.slice_in_dim(block, 0, width, axis=dim), axis, backward)
        block = jnp.concatenate([low, block, high], axis=dim)
    return block


def kernel_blocks(targets, sources):
    radial = jnp.sqrt(targets[0] * targets[0] + targets[1] * targets[1])
    normal_x = (targets[0] / radial)[:, None]
    normal_y = (targets[1] / radial)[:, None]
    delta_x = targets[0][:, None] - sources[0][None, :]
    delta_y = targets[1][:, None] - sources[1][None, :]
    delta_z = targets[2][:, None] - sources[2][None, :]
    areas = sources[3][None, :]
    dist_sq = delta_x * delta_x + delta_y * delta_y + delta_z * delta_z + areas / math.pi
    distance = jnp.sqrt(dist_sq)
    inverse = 1.0 / distance
    phase_arg = wave_number * distance
    cosine = jnp.cos(phase_arg)
    sine_part = jnp.sin(phase_arg)
    weight = areas * (1.0 / (4.0 * math.pi)) * inverse
    single = single_scale * weight
    double = double_scale * weight * (normal_x * delta_x + normal_y * delta_y) * inverse * inverse
    real_stack = jnp.concatenate(
        [single * cosine, double * (-cosine - phase_arg * sine_part)], axis=0
    )
    imag_stack = jnp.concatenate(
        [single * sine_part, double * (phase_arg * cosine - sine_part)], axis=0
    )
    return (real_stack.astype(jnp.bfloat16), imag_stack.astype(jnp.bfloat16))


def form_kernels(targets, sources):
    width = sources.shape[1]
    block_cols = math.gcd(width, 1024)
    block_count = width // block_cols
    source_blocks = jnp.transpose(sources.reshape(4, block_count, block_cols), (1, 0, 2))
    real_blocks, imag_blocks = lax.map(lambda block: kernel_blocks(targets, block), source_blocks)
    rows_out = real_blocks.shape[1]
    real_stack = jnp.transpose(real_blocks, (1, 0, 2)).reshape(rows_out, width)
    imag_stack = jnp.transpose(imag_blocks, (1, 0, 2)).reshape(rows_out, width)
    return (real_stack, imag_stack)


def fold_columns(real_stack, imag_stack):

    def fold_step(running, shard_piece, first_col):
        half = shard_piece.shape[0] // 2
        rotated = jnp.concatenate([-shard_piece[half:], shard_piece[:half]], axis=0)
        first = jnp.einsum("lc,rc->lr", shard_piece, real_stack, preferred_element_type=jnp.float32)
        second = jnp.einsum("lc,rc->lr", rotated, imag_stack, preferred_element_type=jnp.float32)
        return first + second

    return fold_step


def laplace_inner(extended):
    return (
        extended[..., 2:, 1:-1]
        + extended[..., :-2, 1:-1]
        + extended[..., 1:-1, 2:]
        + extended[..., 1:-1, :-2]
        - 4.0 * extended[..., 1:-1, 1:-1]
    )


def clear_outside(extended, width, blk_index, axial):
    total_rows = axial * lax.axis_size("blk")
    rows_here = blk_index * axial - width + jnp.arange(axial + 2 * width, dtype=jnp.int32)
    inside = (rows_here >= 0) & (rows_here < total_rows)
    return jnp.where(inside[:, None], extended, 0.0)


def relax(motion, bend, load, stiffness, hoop_rows):
    half = motion.shape[0] // 2
    shift = hoop_spring * hoop_rows - inertia_term
    applied_re = bend[:half] - loss_factor * bend[half:] + shift * motion[:half]
    applied_im = bend[half:] + loss_factor * bend[:half] + shift * motion[half:]
    resid_re = load[:half] - applied_re
    resid_im = load[half:] - applied_im
    diag_re = 20.0 * stiffness + shift
    diag_im = 20.0 * loss_factor * stiffness
    denom = diag_re * diag_re + diag_im * diag_im
    update_re = (resid_re * diag_re + resid_im * diag_im) / denom
    update_im = (resid_im * diag_re - resid_re * diag_im) / denom
    return motion + relaxation * jnp.concatenate([update_re, update_im], axis=0)


def per_device(
    panels, node_of_panel, stiffener_rows, density_start, motion_start, force, stiffness
):
    panel_dev = panels.shape[1]
    channels = density_start.shape[0]
    axial, circum = stiffness.shape
    blk_index = lax.axis_index("blk")
    devices = lax.axis_size("blk") * lax.axis_size("circ")
    rows_global = blk_index * axial + jnp.arange(axial, dtype=jnp.int32)
    hoop_rows = jnp.any(rows_global[:, None] == stiffener_rows[None, :], axis=1).astype(
        jnp.float32
    )[:, None]
    panel_weight = panels[3] * (panel_dev * devices / (8.0 * math.pi))
    stiff_ext = padded(stiffness, (("blk", 0), ("circ", 1)), 1)
    sources = lax.all_gather(panels, ("blk", "circ"), axis=1, tiled=True)
    target_rows = panels.shape[1]
    real_stack, imag_stack = form_kernels(panels, sources)
    fold_step = fold_columns(real_stack, imag_stack)
    density = density_start
    motion = motion_start
    pressure = jnp.zeros_like(density_start)
    for round_index in range(ITERS):
        flat_motion = motion.reshape(channels, axial * circum)
        neumann = jnp.take(flat_motion, node_of_panel, axis=1)
        density_bf = density.astype(jnp.bfloat16)
        start_sum = jnp.zeros((channels, 2 * target_rows), jnp.float32)
        combined = fold_step(
            start_sum, lax.all_gather(density_bf, ("blk", "circ"), axis=1, tiled=True), jnp.int32(0)
        )
        single_part = combined[:, :target_rows]
        double_part = combined[:, target_rows:]
        pressure = single_part
        density = 0.5 * density + neumann - double_part
        fluid = jnp.zeros((channels, axial * circum), jnp.float32)
        fluid = fluid.at[:, node_of_panel].add(panel_weight[None, :] * pressure)
        load = force - fluid.reshape(channels, axial, circum)
        for sweep_index in range(SWEEPS):
            motion_ext = padded(motion, (("blk", 1), ("circ", 2)), 2)
            motion_ext = clear_outside(motion_ext, 2, blk_index, axial)
            moment = clear_outside(stiff_ext * laplace_inner(motion_ext), 1, blk_index, axial)
            bend = laplace_inner(moment)
            motion = relax(motion, bend, load, stiffness, hoop_rows)
    return (density, pressure, motion)


def solution(mesh):
    in_specs = (
        P(None, ("blk", "circ")),
        P(("blk", "circ")),
        P(),
        P(None, ("blk", "circ")),
        P(None, "blk", "circ"),
        P(None, "blk", "circ"),
        P("blk", "circ"),
    )
    out_specs = (P(None, ("blk", "circ")), P(None, ("blk", "circ")), P(None, "blk", "circ"))
    return jax.shard_map(
        per_device, mesh=mesh, in_specs=in_specs, out_specs=out_specs, check_vma=False
    )
```

profile of v0, /device:TPU:0, one launch (start us, length us, event | category | flops | bytes accessed | tf_op | source)
XLA Modules:
  0.0 319.9 jit_solution(7959979052707602446)
XLA Ops:
  0.6 1.1 fusion.141
  1.7 3.0 collective-permute-start.4
  4.7 3.1 collective-permute-start.5
  7.8 0.8 fusion.143
  8.6 4.7 %collective-permute-start.1 = (f32[1,256]{1,0:T(1,128)S(1)}, f32[1,256]{1,0:T(1,128)S(1)}, u32[]{:S(2)}, u32[]{:S(2)}) collective-permute-start(f32[1,256]{1,0:T(1,128)S(1)} %get-tuple-element.109), channel_id=1, source_target_pairs={{4,0},{8,4},{12,8},{16,12},{20,16},{24,20},{28,24},{0,28},{5,1},{9... | collective-permute-start | bytes 3080 | tf_op jit(solution)/shard_map/ppermute | solution.py:30
  14.0 38.1 %all-gather = f32[32,32,4]{1,2,0:T(4,128)S(1)} all-gather(f32[1,32,4]{1,2,0:T(4,128)S(1)} %bitcast.121), channel_id=1, replica_groups=mesh['blk'=8,'circ'=4] {'blk','circ'}, dimensions={0}, use_global_device_ids=true | all-gather | bytes 16896 | tf_op jit(solution)/shard_map/all_gather | solution.py:131
  52.2 0.7 copy-done.3
  52.9 37.1 %all-gather.1 = bf16[32,32,16]{1,2,0:T(8,128)(2,1)S(1)} all-gather(bf16[1,32,16]{1,2,0:T(8,128)(2,1)S(1)} %convert_bitcast_fusion.3), channel_id=1, replica_groups=mesh['blk'=8,'circ'=4] {'blk','circ'}, dimensions={0}, use_global_device_ids=true | all-gather | bytes 33792 | tf_op jit(solution)/shard_map/all_gather | solution.py:144
  90.8 0.7 multiply_convert_fusion
  91.9 38.2 %all-gather.2 = bf16[32,32,16]{1,2,0:T(8,128)(2,1)S(1)} all-gather(bf16[1,32,16]{1,2,0:T(8,128)(2,1)S(1)} %get-tuple-element.107), channel_id=1, replica_groups=mesh['blk'=8,'circ'=4] {'blk','circ'}, dimensions={0}, use_global_device_ids=true | all-gather | bytes 33792 | tf_op jit(solution)/shard_map/all_gather | solution.py:144
  130.8 1.0 scatter_custom_fusion.1
  132.1 1.0 scatter_custom_fusion
  133.5 0.6 copy-done.6
  134.8 1.4 collective-permute-start.3
  136.5 1.7 collective-permute-start.7
  138.3 3.3 %collective-permute-done.6 = f32[16,12,2]{2,1,0:T(8,128)S(1)} collective-permute-done((f32[16,12,2]{2,1,0:T(8,128)S(1)}, f32[16,12,2]{2,1,0:T(8,128)S(1)}, u32[]{:S(2)}, u32[]{:S(2)}) %collective-permute-start.6) | collective-permute-done | bytes 1568 | tf_op jit(solution)/shard_map/ppermute | solution.py:27
  142.8 4.7 %collective-permute-start.9 = (f32[16,2,256]{2,1,0:T(2,128)S(1)}, f32[16,2,256]{2,1,0:T(2,128)S(1)}, u32[]{:S(2)}, u32[]{:S(2)}) collective-permute-start(f32[16,2,256]{2,1,0:T(2,128)S(1)} %get-tuple-element.82), channel_id=1, source_target_pairs={{4,0},{8,4},{12,8},{16,12},{20,16},{24,20},{28,24},{0,28},{5,1},{9... | collective-permute-start | bytes 98312 | tf_op jit(solution)/shard_map/ppermute | solution.py:30
  147.5 1.9 collective-permute-done.8
  149.6 1.7 collective-permute-start.11
  151.4 3.4 %collective-permute-done.10 = f32[16,12,2]{2,1,0:T(8,128)S(1)} collective-permute-done((f32[16,12,2]{2,1,0:T(8,128)S(1)}, f32[16,12,2]{2,1,0:T(8,128)S(1)}, u32[]{:S(2)}, u32[]{:S(2)}) %collective-permute-start.10) | collective-permute-done | bytes 1568 | tf_op jit(solution)/shard_map/ppermute | solution.py:27
  156.4 4.7 %collective-permute-start.13 = (f32[16,2,256]{2,1,0:T(2,128)S(1)}, f32[16,2,256]{2,1,0:T(2,128)S(1)}, u32[]{:S(2)}, u32[]{:S(2)}) collective-permute-start(f32[16,2,256]{2,1,0:T(2,128)S(1)} %get-tuple-element.80), channel_id=1, source_target_pairs={{4,0},{8,4},{12,8},{16,12},{20,16},{24,20},{28,24},{0,28},{5,1},{9... | collective-permute-start | bytes 98312 | tf_op jit(solution)/shard_map/ppermute | solution.py:30
  161.9 38.2 %all-gather.3 = bf16[32,32,16]{1,2,0:T(8,128)(2,1)S(1)} all-gather(bf16[1,32,16]{1,2,0:T(8,128)(2,1)S(1)} %get-tuple-element.39), channel_id=1, replica_groups=mesh['blk'=8,'circ'=4] {'blk','circ'}, dimensions={0}, use_global_device_ids=true | all-gather | bytes 33792 | tf_op jit(solution)/shard_map/all_gather | solution.py:144
  200.9 1.4 collective-permute-start.15
  202.3 3.3 %collective-permute-done.14 = f32[16,12,2]{2,1,0:T(8,128)S(1)} collective-permute-done((f32[16,12,2]{2,1,0:T(8,128)S(1)}, f32[16,12,2]{2,1,0:T(8,128)S(1)}, u32[]{:S(2)}, u32[]{:S(2)}) %collective-permute-start.14) | collective-permute-done | bytes 1568 | tf_op jit(solution)/shard_map/ppermute | solution.py:27
  206.9 4.7 %collective-permute-start.17 = (f32[16,2,256]{2,1,0:T(2,128)S(1)}, f32[16,2,256]{2,1,0:T(2,128)S(1)}, u32[]{:S(2)}, u32[]{:S(2)}) collective-permute-start(f32[16,2,256]{2,1,0:T(2,128)S(1)} %get-tuple-element.76), channel_id=1, source_target_pairs={{4,0},{8,4},{12,8},{16,12},{20,16},{24,20},{28,24},{0,28},{5,1},{9... | collective-permute-start | bytes 98312 | tf_op jit(solution)/shard_map/ppermute | solution.py:30
  211.7 1.7 collective-permute-done.16
  213.7 1.7 collective-permute-start.19
  215.6 3.3 %collective-permute-done.18 = f32[16,12,2]{2,1,0:T(8,128)S(1)} collective-permute-done((f32[16,12,2]{2,1,0:T(8,128)S(1)}, f32[16,12,2]{2,1,0:T(8,128)S(1)}, u32[]{:S(2)}, u32[]{:S(2)}) %collective-permute-start.18) | collective-permute-done | bytes 1568 | tf_op jit(solution)/shard_map/ppermute | solution.py:27
  221.1 40.9 %all-gather.4 = bf16[32,32,16]{1,2,0:T(8,128)(2,1)S(1)} all-gather(bf16[1,32,16]{1,2,0:T(8,128)(2,1)S(1)} %get-tuple-element.105), channel_id=1, replica_groups=mesh['blk'=8,'circ'=4] {'blk','circ'}, dimensions={0}, use_global_device_ids=true | all-gather | bytes 33792 | tf_op jit(solution)/shard_map/all_gather | solution.py:144
  262.5 4.7 %collective-permute-start.21 = (f32[16,2,256]{2,1,0:T(2,128)S(1)}, f32[16,2,256]{2,1,0:T(2,128)S(1)}, u32[]{:S(2)}, u32[]{:S(2)}) collective-permute-start(f32[16,2,256]{2,1,0:T(2,128)S(1)} %get-tuple-element.74), channel_id=1, source_target_pairs={{4,0},{8,4},{12,8},{16,12},{20,16},{24,20},{28,24},{0,28},{5,1},{9... | collective-permute-start | bytes 98312 | tf_op jit(solution)/shard_map/ppermute | solution.py:30
  268.0 1.0 scatter_custom_fusion.3
  269.4 1.0 scatter_custom_fusion.2
  270.9 1.7 collective-permute-start.23
  272.7 4.0 %collective-permute-done.22 = f32[16,12,2]{2,1,0:T(8,128)S(1)} collective-permute-done((f32[16,12,2]{2,1,0:T(8,128)S(1)}, f32[16,12,2]{2,1,0:T(8,128)S(1)}, u32[]{:S(2)}, u32[]{:S(2)}) %collective-permute-start.22) | collective-permute-done | bytes 1568 | tf_op jit(solution)/shard_map/ppermute | solution.py:27
  277.9 4.7 %collective-permute-start.25 = (f32[16,2,256]{2,1,0:T(2,128)S(1)}, f32[16,2,256]{2,1,0:T(2,128)S(1)}, u32[]{:S(2)}, u32[]{:S(2)}) collective-permute-start(f32[16,2,256]{2,1,0:T(2,128)S(1)} %get-tuple-element.72), channel_id=1, source_target_pairs={{4,0},{8,4},{12,8},{16,12},{20,16},{24,20},{28,24},{0,28},{5,1},{9... | collective-permute-start | bytes 98312 | tf_op jit(solution)/shard_map/ppermute | solution.py:30
  282.7 1.9 collective-permute-done.24
  284.8 1.7 collective-permute-start.27
  286.5 4.0 %collective-permute-done.26 = f32[16,12,2]{2,1,0:T(8,128)S(1)} collective-permute-done((f32[16,12,2]{2,1,0:T(8,128)S(1)}, f32[16,12,2]{2,1,0:T(8,128)S(1)}, u32[]{:S(2)}, u32[]{:S(2)}) %collective-permute-start.26) | collective-permute-done | bytes 1568 | tf_op jit(solution)/shard_map/ppermute | solution.py:27
  291.8 4.7 %collective-permute-start.29 = (f32[16,2,256]{2,1,0:T(2,128)S(1)}, f32[16,2,256]{2,1,0:T(2,128)S(1)}, u32[]{:S(2)}, u32[]{:S(2)}) collective-permute-start(f32[16,2,256]{2,1,0:T(2,128)S(1)} %get-tuple-element.70), channel_id=1, source_target_pairs={{4,0},{8,4},{12,8},{16,12},{20,16},{24,20},{28,24},{0,28},{5,1},{9... | collective-permute-start | bytes 98312 | tf_op jit(solution)/shard_map/ppermute | solution.py:30
  296.5 1.9 collective-permute-done.28
  298.6 1.7 collective-permute-start.31
  300.3 3.9 %collective-permute-done.30 = f32[16,12,2]{2,1,0:T(8,128)S(1)} collective-permute-done((f32[16,12,2]{2,1,0:T(8,128)S(1)}, f32[16,12,2]{2,1,0:T(8,128)S(1)}, u32[]{:S(2)}, u32[]{:S(2)}) %collective-permute-start.30) | collective-permute-done | bytes 1568 | tf_op jit(solution)/shard_map/ppermute | solution.py:27
  305.5 4.8 %collective-permute-start.33 = (f32[16,2,256]{2,1,0:T(2,128)S(1)}, f32[16,2,256]{2,1,0:T(2,128)S(1)}, u32[]{:S(2)}, u32[]{:S(2)}) collective-permute-start(f32[16,2,256]{2,1,0:T(2,128)S(1)} %get-tuple-element.66), channel_id=1, source_target_pairs={{4,0},{8,4},{12,8},{16,12},{20,16},{24,20},{28,24},{0,28},{5,1},{9... | collective-permute-start | bytes 98312 | tf_op jit(solution)/shard_map/ppermute | solution.py:30
  311.4 0.8 collective-permute-done.32
  312.4 1.7 collective-permute-start.35
  314.1 0.7 slice_subtract_fusion
  314.8 3.3 %collective-permute-done.34 = f32[16,12,2]{2,1,0:T(8,128)S(1)} collective-permute-done((f32[16,12,2]{2,1,0:T(8,128)S(1)}, f32[16,12,2]{2,1,0:T(8,128)S(1)}, u32[]{:S(2)}, u32[]{:S(2)}) %collective-permute-start.34) | collective-permute-done | bytes 1568 | tf_op jit(solution)/shard_map/ppermute | solution.py:27
  319.2 0.7 fusion.53
  (187 shorter events, 21.1 us)
Async XLA Ops:
  0.6 12.7 %copy-start = (f32[16,8,256]{2,1,0:T(8,128)S(1)}, f32[16,8,256]{2,1,0:T(8,128)}, u32[]{:S(2)}) copy-start(f32[16,8,256]{2,1,0:T(8,128)} %param.13) | copy-start | bytes 393220
  1.7 134.5 %collective-permute-start.4 = (f32[16,2,256]{2,1,0:T(2,128)S(1)}, f32[16,2,256]{2,1,0:T(2,128)S(1)}, u32[]{:S(2)}, u32[]{:S(2)}) collective-permute-start(f32[16,2,256]{2,1,0:T(2,128)S(1)} %get-tuple-element.83), channel_id=1, source_target_pairs={{0,4},{4,8},{8,12},{12,16},{16,20},{20,24},{24,28},{28,0},{1,5},{5... | collective-permute-start | bytes 98312 | tf_op jit(solution)/shard_map/ppermute | solution.py:27
  4.7 131.5 %collective-permute-start.5 = (f32[16,2,256]{2,1,0:T(2,128)S(1)}, f32[16,2,256]{2,1,0:T(2,128)S(1)}, u32[]{:S(2)}, u32[]{:S(2)}) collective-permute-start(f32[16,2,256]{2,1,0:T(2,128)S(1)} %get-tuple-element.84), channel_id=1, source_target_pairs={{4,0},{8,4},{12,8},{16,12},{20,16},{24,20},{28,24},{0,28},{5,1},{9... | collective-permute-start | bytes 98312 | tf_op jit(solution)/shard_map/ppermute | solution.py:30
  8.6 4.7 %copy-start.4 = (f32[4,32]{1,0:T(4,128)S(1)}, f32[4,32]{1,0:T(4,128)}, u32[]{:S(2)}) copy-start(f32[4,32]{1,0:T(4,128)} %param.9) | copy-start | bytes 1540
  8.6 125.8 %collective-permute-start = (f32[1,256]{1,0:T(1,128)S(1)}, f32[1,256]{1,0:T(1,128)S(1)}, u32[]{:S(2)}, u32[]{:S(2)}) collective-permute-start(f32[1,256]{1,0:T(1,128)S(1)} %get-tuple-element.108), channel_id=1, source_target_pairs={{0,4},{4,8},{8,12},{12,16},{16,20},{20,24},{24,28},{28,0},{1,5},{5... | collective-permute-start | bytes 3080 | tf_op jit(solution)/shard_map/ppermute | solution.py:27
  8.6 125.8 %collective-permute-start.1 = (f32[1,256]{1,0:T(1,128)S(1)}, f32[1,256]{1,0:T(1,128)S(1)}, u32[]{:S(2)}, u32[]{:S(2)}) collective-permute-start(f32[1,256]{1,0:T(1,128)S(1)} %get-tuple-element.109), channel_id=1, source_target_pairs={{4,0},{8,4},{12,8},{16,12},{20,16},{24,20},{28,24},{0,28},{5,1},{9... | collective-permute-start | bytes 3080 | tf_op jit(solution)/shard_map/ppermute | solution.py:30
  13.4 0.7 copy-start.5
  52.2 0.7 copy-start.3
  133.1 1.2 copy-start.1
  133.5 0.8 copy-start.2
  133.5 0.7 copy-start.6
  134.5 3.7 %collective-permute-start.2 = (f32[10,1]{1,0:T(8,128)S(1)}, f32[10,1]{1,0:T(8,128)S(1)}, u32[]{:S(2)}, u32[]{:S(2)}) collective-permute-start(f32[10,1]{1,0:T(8,128)S(1)} %get-tuple-element.97), channel_id=1, source_target_pairs={{0,1},{1,2},{2,3},{3,0},{4,5},{5,6},{6,7},{7,4},{8,9},{9,10},{10,1... | collective-permute-start | bytes 128 | tf_op jit(solution)/shard_map/ppermute | solution.py:27
  134.8 3.4 %collective-permute-start.3 = (f32[10,1]{1,0:T(8,128)S(1)}, f32[10,1]{1,0:T(8,128)S(1)}, u32[]{:S(2)}, u32[]{:S(2)}) collective-permute-start(f32[10,1]{1,0:T(8,128)S(1)} %get-tuple-element.98), channel_id=1, source_target_pairs={{1,0},{2,1},{3,2},{0,3},{5,4},{6,5},{7,6},{4,7},{9,8},{10,9},{11,1... | collective-permute-start | bytes 128 | tf_op jit(solution)/shard_map/ppermute | solution.py:30
  136.4 5.2 %collective-permute-start.6 = (f32[16,12,2]{2,1,0:T(8,128)S(1)}, f32[16,12,2]{2,1,0:T(8,128)S(1)}, u32[]{:S(2)}, u32[]{:S(2)}) collective-permute-start(f32[16,12,2]{2,1,0:T(8,128)S(1)} %get-tuple-element.63), channel_id=1, source_target_pairs={{0,1},{1,2},{2,3},{3,0},{4,5},{5,6},{6,7},{7,4},{8,9},{9,10},{10,1... | collective-permute-start | bytes 4616 | tf_op jit(solution)/shard_map/ppermute | solution.py:27
  136.5 5.1 %collective-permute-start.7 = (f32[16,12,2]{2,1,0:T(8,128)S(1)}, f32[16,12,2]{2,1,0:T(8,128)S(1)}, u32[]{:S(2)}, u32[]{:S(2)}) collective-permute-start(f32[16,12,2]{2,1,0:T(8,128)S(1)} %get-tuple-element.64), channel_id=1, source_target_pairs={{1,0},{2,1},{3,2},{0,3},{5,4},{6,5},{7,6},{4,7},{9,8},{10,9},{11,1... | collective-permute-start | bytes 4616 | tf_op jit(solution)/shard_map/ppermute | solution.py:30
  142.8 6.7 %collective-permute-start.8 = (f32[16,2,256]{2,1,0:T(2,128)S(1)}, f32[16,2,256]{2,1,0:T(2,128)S(1)}, u32[]{:S(2)}, u32[]{:S(2)}) collective-permute-start(f32[16,2,256]{2,1,0:T(2,128)S(1)} %get-tuple-element.81), channel_id=1, source_target_pairs={{0,4},{4,8},{8,12},{12,16},{16,20},{20,24},{24,28},{28,0},{1,5},{5... | collective-permute-start | bytes 98312 | tf_op jit(solution)/shard_map/ppermute | solution.py:27
  142.8 6.6 %collective-permute-start.9 = (f32[16,2,256]{2,1,0:T(2,128)S(1)}, f32[16,2,256]{2,1,0:T(2,128)S(1)}, u32[]{:S(2)}, u32[]{:S(2)}) collective-permute-start(f32[16,2,256]{2,1,0:T(2,128)S(1)} %get-tuple-element.82), channel_id=1, source_target_pairs={{4,0},{8,4},{12,8},{16,12},{20,16},{24,20},{28,24},{0,28},{5,1},{9... | collective-permute-start | bytes 98312 | tf_op jit(solution)/shard_map/ppermute | solution.py:30
  149.6 5.2 %collective-permute-start.10 = (f32[16,12,2]{2,1,0:T(8,128)S(1)}, f32[16,12,2]{2,1,0:T(8,128)S(1)}, u32[]{:S(2)}, u32[]{:S(2)}) collective-permute-start(f32[16,12,2]{2,1,0:T(8,128)S(1)} %get-tuple-element.61), channel_id=1, source_target_pairs={{0,1},{1,2},{2,3},{3,0},{4,5},{5,6},{6,7},{7,4},{8,9},{9,10},{10,1... | collective-permute-start | bytes 4616 | tf_op jit(solution)/shard_map/ppermute | solution.py:27
  149.6 5.2 %collective-permute-start.11 = (f32[16,12,2]{2,1,0:T(8,128)S(1)}, f32[16,12,2]{2,1,0:T(8,128)S(1)}, u32[]{:S(2)}, u32[]{:S(2)}) collective-permute-start(f32[16,12,2]{2,1,0:T(8,128)S(1)} %get-tuple-element.62), channel_id=1, source_target_pairs={{1,0},{2,1},{3,2},{0,3},{5,4},{6,5},{7,6},{4,7},{9,8},{10,9},{11,1... | collective-permute-start | bytes 4616 | tf_op jit(solution)/shard_map/ppermute | solution.py:30
  156.4 43.9 %collective-permute-start.12 = (f32[16,2,256]{2,1,0:T(2,128)S(1)}, f32[16,2,256]{2,1,0:T(2,128)S(1)}, u32[]{:S(2)}, u32[]{:S(2)}) collective-permute-start(f32[16,2,256]{2,1,0:T(2,128)S(1)} %get-tuple-element.79), channel_id=1, source_target_pairs={{0,4},{4,8},{8,12},{12,16},{16,20},{20,24},{24,28},{28,0},{1,5},{5... | collective-permute-start | bytes 98312 | tf_op jit(solution)/shard_map/ppermute | solution.py:27
  156.4 43.9 %collective-permute-start.13 = (f32[16,2,256]{2,1,0:T(2,128)S(1)}, f32[16,2,256]{2,1,0:T(2,128)S(1)}, u32[]{:S(2)}, u32[]{:S(2)}) collective-permute-start(f32[16,2,256]{2,1,0:T(2,128)S(1)} %get-tuple-element.80), channel_id=1, source_target_pairs={{4,0},{8,4},{12,8},{16,12},{20,16},{24,20},{28,24},{0,28},{5,1},{9... | collective-permute-start | bytes 98312 | tf_op jit(solution)/shard_map/ppermute | solution.py:30
  200.5 5.1 %collective-permute-start.14 = (f32[16,12,2]{2,1,0:T(8,128)S(1)}, f32[16,12,2]{2,1,0:T(8,128)S(1)}, u32[]{:S(2)}, u32[]{:S(2)}) collective-permute-start(f32[16,12,2]{2,1,0:T(8,128)S(1)} %get-tuple-element.59), channel_id=1, source_target_pairs={{0,1},{1,2},{2,3},{3,0},{4,5},{5,6},{6,7},{7,4},{8,9},{9,10},{10,1... | collective-permute-start | bytes 4616 | tf_op jit(solution)/shard_map/ppermute | solution.py:27
  200.9 4.7 %collective-permute-start.15 = (f32[16,12,2]{2,1,0:T(8,128)S(1)}, f32[16,12,2]{2,1,0:T(8,128)S(1)}, u32[]{:S(2)}, u32[]{:S(2)}) collective-permute-start(f32[16,12,2]{2,1,0:T(8,128)S(1)} %get-tuple-element.60), channel_id=1, source_target_pairs={{1,0},{2,1},{3,2},{0,3},{5,4},{6,5},{7,6},{4,7},{9,8},{10,9},{11,1... | collective-permute-start | bytes 4616 | tf_op jit(solution)/shard_map/ppermute | solution.py:30
  206.8 6.7 %collective-permute-start.16 = (f32[16,2,256]{2,1,0:T(2,128)S(1)}, f32[16,2,256]{2,1,0:T(2,128)S(1)}, u32[]{:S(2)}, u32[]{:S(2)}) collective-permute-start(f32[16,2,256]{2,1,0:T(2,128)S(1)} %get-tuple-element.75), channel_id=1, source_target_pairs={{0,4},{4,8},{8,12},{12,16},{16,20},{20,24},{24,28},{28,0},{1,5},{5... | collective-permute-start | bytes 98312 | tf_op jit(solution)/shard_map/ppermute | solution.py:27
  206.9 6.6 %collective-permute-start.17 = (f32[16,2,256]{2,1,0:T(2,128)S(1)}, f32[16,2,256]{2,1,0:T(2,128)S(1)}, u32[]{:S(2)}, u32[]{:S(2)}) collective-permute-start(f32[16,2,256]{2,1,0:T(2,128)S(1)} %get-tuple-element.76), channel_id=1, source_target_pairs={{4,0},{8,4},{12,8},{16,12},{20,16},{24,20},{28,24},{0,28},{5,1},{9... | collective-permute-start | bytes 98312 | tf_op jit(solution)/shard_map/ppermute | solution.py:30
  213.6 5.2 %collective-permute-start.18 = (f32[16,12,2]{2,1,0:T(8,128)S(1)}, f32[16,12,2]{2,1,0:T(8,128)S(1)}, u32[]{:S(2)}, u32[]{:S(2)}) collective-permute-start(f32[16,12,2]{2,1,0:T(8,128)S(1)} %get-tuple-element.57), channel_id=1, source_target_pairs={{0,1},{1,2},{2,3},{3,0},{4,5},{5,6},{6,7},{7,4},{8,9},{9,10},{10,1... | collective-permute-start | bytes 4616 | tf_op jit(solution)/shard_map/ppermute | solution.py:27
  213.7 5.2 %collective-permute-start.19 = (f32[16,12,2]{2,1,0:T(8,128)S(1)}, f32[16,12,2]{2,1,0:T(8,128)S(1)}, u32[]{:S(2)}, u32[]{:S(2)}) collective-permute-start(f32[16,12,2]{2,1,0:T(8,128)S(1)} %get-tuple-element.58), channel_id=1, source_target_pairs={{1,0},{2,1},{3,2},{0,3},{5,4},{6,5},{7,6},{4,7},{9,8},{10,9},{11,1... | collective-permute-start | bytes 4616 | tf_op jit(solution)/shard_map/ppermute | solution.py:30
  262.4 8.2 %collective-permute-start.20 = (f32[16,2,256]{2,1,0:T(2,128)S(1)}, f32[16,2,256]{2,1,0:T(2,128)S(1)}, u32[]{:S(2)}, u32[]{:S(2)}) collective-permute-start(f32[16,2,256]{2,1,0:T(2,128)S(1)} %get-tuple-element.73), channel_id=1, source_target_pairs={{0,4},{4,8},{8,12},{12,16},{16,20},{20,24},{24,28},{28,0},{1,5},{5... | collective-permute-start | bytes 98312 | tf_op jit(solution)/shard_map/ppermute | solution.py:27
  262.5 8.2 %collective-permute-start.21 = (f32[16,2,256]{2,1,0:T(2,128)S(1)}, f32[16,2,256]{2,1,0:T(2,128)S(1)}, u32[]{:S(2)}, u32[]{:S(2)}) collective-permute-start(f32[16,2,256]{2,1,0:T(2,128)S(1)} %get-tuple-element.74), channel_id=1, source_target_pairs={{4,0},{8,4},{12,8},{16,12},{20,16},{24,20},{28,24},{0,28},{5,1},{9... | collective-permute-start | bytes 98312 | tf_op jit(solution)/shard_map/ppermute | solution.py:30
  270.9 5.8 %collective-permute-start.22 = (f32[16,12,2]{2,1,0:T(8,128)S(1)}, f32[16,12,2]{2,1,0:T(8,128)S(1)}, u32[]{:S(2)}, u32[]{:S(2)}) collective-permute-start(f32[16,12,2]{2,1,0:T(8,128)S(1)} %get-tuple-element.55), channel_id=1, source_target_pairs={{0,1},{1,2},{2,3},{3,0},{4,5},{5,6},{6,7},{7,4},{8,9},{9,10},{10,1... | collective-permute-start | bytes 4616 | tf_op jit(solution)/shard_map/ppermute | solution.py:27
  270.9 5.8 %collective-permute-start.23 = (f32[16,12,2]{2,1,0:T(8,128)S(1)}, f32[16,12,2]{2,1,0:T(8,128)S(1)}, u32[]{:S(2)}, u32[]{:S(2)}) collective-permute-start(f32[16,12,2]{2,1,0:T(8,128)S(1)} %get-tuple-element.56), channel_id=1, source_target_pairs={{1,0},{2,1},{3,2},{0,3},{5,4},{6,5},{7,6},{4,7},{9,8},{10,9},{11,1... | collective-permute-start | bytes 4616 | tf_op jit(solution)/shard_map/ppermute | solution.py:30
  277.9 6.7 %collective-permute-start.24 = (f32[16,2,256]{2,1,0:T(2,128)S(1)}, f32[16,2,256]{2,1,0:T(2,128)S(1)}, u32[]{:S(2)}, u32[]{:S(2)}) collective-permute-start(f32[16,2,256]{2,1,0:T(2,128)S(1)} %get-tuple-element.71), channel_id=1, source_target_pairs={{0,4},{4,8},{8,12},{12,16},{16,20},{20,24},{24,28},{28,0},{1,5},{5... | collective-permute-start | bytes 98312 | tf_op jit(solution)/shard_map/ppermute | solution.py:27
  277.9 6.6 %collective-permute-start.25 = (f32[16,2,256]{2,1,0:T(2,128)S(1)}, f32[16,2,256]{2,1,0:T(2,128)S(1)}, u32[]{:S(2)}, u32[]{:S(2)}) collective-permute-start(f32[16,2,256]{2,1,0:T(2,128)S(1)} %get-tuple-element.72), channel_id=1, source_target_pairs={{4,0},{8,4},{12,8},{16,12},{20,16},{24,20},{28,24},{0,28},{5,1},{9... | collective-permute-start | bytes 98312 | tf_op jit(solution)/shard_map/ppermute | solution.py:30
  284.7 5.8 %collective-permute-start.26 = (f32[16,12,2]{2,1,0:T(8,128)S(1)}, f32[16,12,2]{2,1,0:T(8,128)S(1)}, u32[]{:S(2)}, u32[]{:S(2)}) collective-permute-start(f32[16,12,2]{2,1,0:T(8,128)S(1)} %get-tuple-element.53), channel_id=1, source_target_pairs={{0,1},{1,2},{2,3},{3,0},{4,5},{5,6},{6,7},{7,4},{8,9},{9,10},{10,1... | collective-permute-start | bytes 4616 | tf_op jit(solution)/shard_map/ppermute | solution.py:27
  284.8 5.8 %collective-permute-start.27 = (f32[16,12,2]{2,1,0:T(8,128)S(1)}, f32[16,12,2]{2,1,0:T(8,128)S(1)}, u32[]{:S(2)}, u32[]{:S(2)}) collective-permute-start(f32[16,12,2]{2,1,0:T(8,128)S(1)} %get-tuple-element.54), channel_id=1, source_target_pairs={{1,0},{2,1},{3,2},{0,3},{5,4},{6,5},{7,6},{4,7},{9,8},{10,9},{11,1... | collective-permute-start | bytes 4616 | tf_op jit(solution)/shard_map/ppermute | solution.py:30
  291.7 6.7 %collective-permute-start.28 = (f32[16,2,256]{2,1,0:T(2,128)S(1)}, f32[16,2,256]{2,1,0:T(2,128)S(1)}, u32[]{:S(2)}, u32[]{:S(2)}) collective-permute-start(f32[16,2,256]{2,1,0:T(2,128)S(1)} %get-tuple-element.69), channel_id=1, source_target_pairs={{0,4},{4,8},{8,12},{12,16},{16,20},{20,24},{24,28},{28,0},{1,5},{5... | collective-permute-start | bytes 98312 | tf_op jit(solution)/shard_map/ppermute | solution.py:27
  291.8 6.6 %collective-permute-start.29 = (f32[16,2,256]{2,1,0:T(2,128)S(1)}, f32[16,2,256]{2,1,0:T(2,128)S(1)}, u32[]{:S(2)}, u32[]{:S(2)}) collective-permute-start(f32[16,2,256]{2,1,0:T(2,128)S(1)} %get-tuple-element.70), channel_id=1, source_target_pairs={{4,0},{8,4},{12,8},{16,12},{20,16},{24,20},{28,24},{0,28},{5,1},{9... | collective-permute-start | bytes 98312 | tf_op jit(solution)/shard_map/ppermute | solution.py:30
  298.5 5.7 %collective-permute-start.30 = (f32[16,12,2]{2,1,0:T(8,128)S(1)}, f32[16,12,2]{2,1,0:T(8,128)S(1)}, u32[]{:S(2)}, u32[]{:S(2)}) collective-permute-start(f32[16,12,2]{2,1,0:T(8,128)S(1)} %get-tuple-element.51), channel_id=1, source_target_pairs={{0,1},{1,2},{2,3},{3,0},{4,5},{5,6},{6,7},{7,4},{8,9},{9,10},{10,1... | collective-permute-start | bytes 4616 | tf_op jit(solution)/shard_map/ppermute | solution.py:27
  298.6 5.7 %collective-permute-start.31 = (f32[16,12,2]{2,1,0:T(8,128)S(1)}, f32[16,12,2]{2,1,0:T(8,128)S(1)}, u32[]{:S(2)}, u32[]{:S(2)}) collective-permute-start(f32[16,12,2]{2,1,0:T(8,128)S(1)} %get-tuple-element.52), channel_id=1, source_target_pairs={{1,0},{2,1},{3,2},{0,3},{5,4},{6,5},{7,6},{4,7},{9,8},{10,9},{11,1... | collective-permute-start | bytes 4616 | tf_op jit(solution)/shard_map/ppermute | solution.py:30
  305.5 6.7 %collective-permute-start.32 = (f32[16,2,256]{2,1,0:T(2,128)S(1)}, f32[16,2,256]{2,1,0:T(2,128)S(1)}, u32[]{:S(2)}, u32[]{:S(2)}) collective-permute-start(f32[16,2,256]{2,1,0:T(2,128)S(1)} %get-tuple-element.65), channel_id=1, source_target_pairs={{0,4},{4,8},{8,12},{12,16},{16,20},{20,24},{24,28},{28,0},{1,5},{5... | collective-permute-start | bytes 98312 | tf_op jit(solution)/shard_map/ppermute | solution.py:27
  305.5 6.6 %collective-permute-start.33 = (f32[16,2,256]{2,1,0:T(2,128)S(1)}, f32[16,2,256]{2,1,0:T(2,128)S(1)}, u32[]{:S(2)}, u32[]{:S(2)}) collective-permute-start(f32[16,2,256]{2,1,0:T(2,128)S(1)} %get-tuple-element.66), channel_id=1, source_target_pairs={{4,0},{8,4},{12,8},{16,12},{20,16},{24,20},{28,24},{0,28},{5,1},{9... | collective-permute-start | bytes 98312 | tf_op jit(solution)/shard_map/ppermute | solution.py:30
  312.3 5.8 %collective-permute-start.34 = (f32[16,12,2]{2,1,0:T(8,128)S(1)}, f32[16,12,2]{2,1,0:T(8,128)S(1)}, u32[]{:S(2)}, u32[]{:S(2)}) collective-permute-start(f32[16,12,2]{2,1,0:T(8,128)S(1)} %get-tuple-element.49), channel_id=1, source_target_pairs={{0,1},{1,2},{2,3},{3,0},{4,5},{5,6},{6,7},{7,4},{8,9},{9,10},{10,1... | collective-permute-start | bytes 4616 | tf_op jit(solution)/shard_map/ppermute | solution.py:27
  312.4 5.7 %collective-permute-start.35 = (f32[16,12,2]{2,1,0:T(8,128)S(1)}, f32[16,12,2]{2,1,0:T(8,128)S(1)}, u32[]{:S(2)}, u32[]{:S(2)}) collective-permute-start(f32[16,12,2]{2,1,0:T(8,128)S(1)} %get-tuple-element.50), channel_id=1, source_target_pairs={{1,0},{2,1},{3,2},{0,3},{5,4},{6,5},{7,6},{4,7},{9,8},{10,9},{11,1... | collective-permute-start | bytes 4616 | tf_op jit(solution)/shard_map/ppermute | solution.py:30
where the time goes:
time: 320 us
  blocking collectives  193 us (60%)
  starting transfers between devices  60.4 us (19%)
  waiting for transfers between devices  36.9 us (12%)
  other arithmetic  16.6 us (5%)
  local copies, waits for them, and re-layouts  10.9 us (3%)
    all_gather x4, blocking collectives, per_device(): lax.all_gather(density_bf, ('blk', 'circ'), axis=1, tiled=True)  154 us
    ppermute x18, starting transfers between devices, padded(): lax.ppermute(lax.slice_in_dim(block, 0, width, axis=dim), axis, backward)  55.8 us
    all_gather x1, blocking collectives, per_device(): sources = lax.all_gather(panels, ('blk', 'circ'), axis=1, tiled=True)  38.1 us
    ppermute x18, waiting for transfers between devices, padded(): lax.ppermute(lax.slice_in_dim(block, block.shape[dim] - width, None, axis...  36.8 us
  transfers between devices with their start and end apart: 36, of which 13 were waited for; matrix products, arithmetic and copies ran while one was open for 4% of the time, Pallas kernels for 0%

commit v1 on v0

v1 whole, which is shorter than its diff:
```python
import functools
import math

import jax
import jax.numpy as jnp
from jax import lax
from jax.experimental import pallas as pl
from jax.experimental.pallas import tpu as pltpu
from jax.sharding import PartitionSpec as P

MESH = pl.DeviceIdType.MESH
ITERS = 4
SWEEPS = 2
STEPS = ITERS * SWEEPS

wave_number = 4.0
single_scale = 30.0
double_scale = 6.0
hoop_spring = 40.0
inertia_term = 4.0
loss_factor = 0.2
relaxation = 0.3

COS = (
    0.9999999890590228, -19.739204499454, 64.93911745989914, -85.45013953093448,
    60.16763095128989, -25.96759924954187, 6.528658162606979,
)
SIN = (
    6.283185302511502, -41.34170040531754, 81.6051313857969, -76.70301535383193,
    42.02592698564183, -14.899846667160109, 3.2381375090822355,
)

UP, DOWN, LEFT, RIGHT, UL, UR, DL, DR = range(8)
OPPOSITE = {UP: DOWN, DOWN: UP, LEFT: RIGHT, RIGHT: LEFT, UL: DR, UR: DL, DL: UR, DR: UL}


def poly(coefs, x):
    acc = jnp.full_like(x, coefs[-1])
    for c in coefs[-2::-1]:
        acc = acc * x + c
    return acc


def split(x):
    high = x.astype(jnp.bfloat16)
    low = (x - high.astype(jnp.float32)).astype(jnp.bfloat16)
    return high, low


def dot(a, b, dims):
    return lax.dot_general(a, b, (dims, ((), ())), preferred_element_type=jnp.float32)


def kernel(
    nb, nc, pd,
    panels, node, hoops, density_in, motion_in, force_in, stiff,
    density_out, pressure_out, motion_out,
    mot, frc, rows_in, cols_in, cols_own, stiff_in, kext, coef, onehot, rowhot,
    dens, press, wide, ga, gb, ga_src, pa, pb, pa_src, mats,
    sh_send, sh_recv, st_send, st_recv, a_send, a_recv, b_send, b_recv, pan_send, pan_recv,
):
    f32 = jnp.float32
    b = lax.axis_index("blk")
    c = lax.axis_index("circ")
    axial, circum = stiff.shape
    last_tile = circum - 128
    cleft, cright = lax.rem(c + nc - 1, nc), lax.rem(c + 1, nc)
    where_to = {
        UP: (b - 1, c), DOWN: (b + 1, c), LEFT: (b, cleft), RIGHT: (b, cright),
        UL: (b - 1, cleft), UR: (b - 1, cright), DL: (b + 1, cleft), DR: (b + 1, cright),
    }
    has_up, has_down = b > 0, b < nb - 1

    def for_dirs(fn):
        fn(LEFT)
        fn(RIGHT)

        @pl.when(has_up)
        def _():
            for d in (UP, UL, UR):
                fn(d)

        @pl.when(has_down)
        def _():
            for d in (DOWN, DL, DR):
                fn(d)

    def for_peers(fn):
        if nb <= 8:
            for j in range(1, nb):
                fn(lax.rem(b + j, nb))
        else:
            def body(j, _):
                fn(lax.rem(b + j, nb))
                return 0

            lax.fori_loop(1, nb, body, 0)

    @pl.when(jnp.logical_not(has_up))
    def _():
        rows_in[:, 0] = jnp.zeros_like(rows_in[:, 0])
        cols_in[:, UL - 2] = jnp.zeros_like(cols_in[:, UL - 2])
        cols_in[:, UR - 2] = jnp.zeros_like(cols_in[:, UR - 2])
        stiff_in[UP] = jnp.zeros_like(stiff_in[UP])

    @pl.when(jnp.logical_not(has_down))
    def _():
        rows_in[:, 1] = jnp.zeros_like(rows_in[:, 1])
        cols_in[:, DL - 2] = jnp.zeros_like(cols_in[:, DL - 2])
        cols_in[:, DR - 2] = jnp.zeros_like(cols_in[:, DR - 2])
        stiff_in[DOWN] = jnp.zeros_like(stiff_in[DOWN])

    barrier = pltpu.get_barrier_semaphore()

    def greet(device):
        pl.semaphore_signal(barrier, inc=1, device_id=device, device_id_type=MESH)

    for j in range(1, nc):
        greet((b, lax.rem(c + j, nc)))
    for_peers(lambda peer: greet((peer, c)))

    @pl.when(has_up)
    def _():
        greet(where_to[UL])
        greet(where_to[UR])

    @pl.when(has_down)
    def _():
        greet(where_to[DL])
        greet(where_to[DR])

    lane = lax.broadcasted_iota(jnp.int32, (16, 128), 1)
    lane8 = lane[:8]

    def spread(x):
        x = jnp.where(lane[: x.shape[0]] < pd, x, 0.0)
        step = pd
        while step < 128:
            x = x + pltpu.roll(x, step, 1)
            step *= 2
        return x

    wide[...] = jnp.zeros_like(wide)
    wide[0:4, 0:pd] = panels[...]
    wide[8:24, 0:pd] = density_in[...]
    own = spread(wide[0:8, :])
    dens[...] = spread(wide[8:24, :])
    pa_src[...] = own
    ga_src[0] = dens[...].astype(jnp.bfloat16)

    pl.semaphore_wait(
        barrier,
        (nc - 1) + (nb - 1) + 2 * has_up.astype(jnp.int32) + 2 * has_down.astype(jnp.int32),
    )

    def copy(src, dst, send, recv, device):
        return pltpu.make_async_remote_copy(
            src_ref=src, dst_ref=dst, send_sem=send, recv_sem=recv,
            device_id=device, device_id_type=MESH,
        )

    me = (b, c)

    def a_start(rnd):
        for j in range(1, nc):
            copy(ga_src.at[rnd], ga.at[rnd, j - 1], a_send.at[rnd, j - 1], a_recv.at[rnd, j - 1],
                 (b, lax.rem(c + j, nc))).start()

    def a_wait(rnd):
        for j in range(1, nc):
            copy(ga_src.at[rnd], ga.at[rnd, j - 1], a_send.at[rnd, j - 1], a_recv.at[rnd, j - 1],
                 me).wait_recv()

    def merge(own_block, parts):
        group = lane[: own_block.shape[0]] // pd
        out = own_block
        for j in range(1, nc):
            out = jnp.where(group == lax.rem(c + nc - j, nc), parts[j - 1], out)
        return out

    def b_start(rnd):
        parts = [ga[rnd, j].astype(f32) for j in range(nc - 1)]
        gb[rnd, b] = merge(ga_src[rnd].astype(f32), parts).astype(jnp.bfloat16)
        for_peers(lambda peer: copy(gb.at[rnd, b], gb.at[rnd, b], b_send.at[rnd], b_recv.at[rnd],
                                    (peer, c)).start())

    def b_all(rnd):
        part = gb.at[rnd, pl.ds(0, nb - 1)]
        return copy(part, part, b_send.at[rnd], b_recv.at[rnd], me)

    for j in range(1, nc):
        copy(pa_src, pa.at[j - 1], pan_send.at[j - 1], pan_recv.at[j - 1],
             (b, lax.rem(c + j, nc))).start()
    a_start(0)
    stiff_dirs = (UP, DOWN, LEFT, RIGHT)

    def stiff_copy(d):
        return copy(stiff, stiff_in.at[OPPOSITE[d]], st_send.at[d], st_recv.at[OPPOSITE[d]],
                    where_to[d])

    for_dirs(lambda d: stiff_copy(d).start() if d in stiff_dirs else None)

    def shell_copy(s, d):
        o = OPPOSITE[d]
        if d in (UP, DOWN):
            src = mot.at[s, pl.ds(0 if d == UP else axial - 2, 2)]
            dst = rows_in.at[s, 0 if o == UP else 1]
        else:
            src, dst = cols_own.at[s], cols_in.at[s, o - 2]
        return copy(src, dst, sh_send.at[s, d], sh_recv.at[s, o], where_to[d])

    def shell_recv(s, d):
        if d in (UP, DOWN):
            dst = rows_in.at[s, 0 if d == UP else 1]
        else:
            dst = cols_in.at[s, d - 2]
        return copy(dst, dst, sh_send.at[s, d], sh_recv.at[s, d], me)

    place = (lane + 2) & 127
    row_of = ((128 - (place - (place & 3))) & 127) // 4

    def shell_start(s, rows):
        packed = None
        for r in range(axial):
            edge = jnp.where(lane < 64, rows[r][:, :128], rows[r][:, last_tile:])
            edge = pltpu.roll(edge, (128 - 4 * r) % 128, 1) if r else edge
            packed = edge if r == 0 else jnp.where(row_of == r, edge, packed)
        cols_own[s] = packed
        for_dirs(lambda d: shell_copy(s, d).start())

    first = []
    for r in range(axial):
        row = motion_in[:, r, :]
        mot[0, r] = row
        first.append(row)
    shell_start(0, first)
    for r in range(axial):
        frc[r] = force_in[:, r, :]

    sub = lax.broadcasted_iota(jnp.int32, (axial, circum), 0) + b * axial
    hoop = jnp.zeros((axial, circum), f32)
    for h in range(hoops.shape[0]):
        hoop = jnp.where(sub == hoops[h], 1.0, hoop)
    k = stiff[...]
    shift = hoop_spring * hoop - inertia_term
    diag_re = 20.0 * k + shift
    diag_im = (20.0 * loss_factor) * k
    scale = relaxation / (diag_re * diag_re + diag_im * diag_im)
    inv_re, inv_im = diag_re * scale, diag_im * scale
    for r in range(axial):
        for n, x in enumerate((shift, inv_re, inv_im)):
            coef[n, r] = jnp.broadcast_to(x[r : r + 1], (8, circum))

    nodes = jnp.zeros((8, 128), jnp.int32)
    for p in range(pd):
        nodes = jnp.where((lane8 & (pd - 1)) == p, node[p], nodes)
    node_row = nodes // circum
    node_col = nodes - node_row * circum
    rowhot[...] = (node_row == lax.broadcasted_iota(jnp.int32, (8, 128), 0)).astype(f32)
    col_iota = lax.broadcasted_iota(jnp.int32, (circum, 128), 0)
    onehot[...] = (
        (jnp.broadcast_to(node_col[0:1], (circum, 128)) == col_iota).astype(f32).astype(jnp.bfloat16)
    )

    for j in range(1, nc):
        copy(pa_src, pa.at[j - 1], pan_send.at[j - 1], pan_recv.at[j - 1], me).wait_recv()
    a_wait(0)
    pb[b] = merge(pa_src[...], [pa[j] for j in range(nc - 1)])
    for_peers(lambda peer: copy(pb.at[b], pb.at[b], pan_send.at[nc - 1], pan_recv.at[nc - 1],
                                (peer, c)).start())
    b_start(0)
    pb_part = pb.at[pl.ds(0, nb - 1)]
    pb_all = copy(pb_part, pb_part, pan_send.at[nc - 1], pan_recv.at[nc - 1], me)

    for_dirs(
        lambda d: copy(stiff_in.at[d], stiff_in.at[d], st_send.at[d], st_recv.at[d], me).wait_recv()
        if d in stiff_dirs else None
    )
    right_tile = stiff_in[RIGHT][:, :128]
    left_tile = stiff_in[LEFT][:, last_tile:]
    side = jnp.where(lane8 < 64, right_tile, left_tile)
    k_up, k_down = stiff_in[UP], stiff_in[DOWN]
    for r in range(axial + 2):
        if r == 0:
            line = k_up[axial - 1 : axial]
        elif r == axial + 1:
            line = k_down[0:1]
        else:
            line = k[r - 1 : r]
            kext[r, :, circum:] = jnp.broadcast_to(side[r - 1 : r], (16, 128))
        kext[r, :, :circum] = jnp.broadcast_to(line, (16, circum))

    radial = jnp.sqrt(own[0:1] * own[0:1] + own[1:2] * own[1:2])
    eye = lax.broadcasted_iota(jnp.int32, (pd, 128), 0) == lax.broadcasted_iota(
        jnp.int32, (pd, 128), 1
    )

    def column(line):
        return jnp.sum(jnp.where(eye, jnp.broadcast_to(line, (pd, 128)), 0.0), axis=1, keepdims=True)

    tx, ty, tz = column(own[0:1]), column(own[1:2]), column(own[2:3])
    nx, ny = column(own[0:1] / radial), column(own[1:2] / radial)
    weight_row = own[3:4] * (pd * nb * nc / (8.0 * math.pi))

    pb_all.wait_recv()

    per = mats.shape[2] // 128
    for q in range(nb // per):
        for i in range(per):
            src = pb[q * per + i]
            dx, dy, dz = tx - src[0:1], ty - src[1:2], tz - src[2:3]
            area = src[3:4]
            dist_sq = dx * dx + dy * dy + dz * dz + area * (1.0 / math.pi)
            inverse = lax.rsqrt(dist_sq)
            phase = (wave_number * dist_sq) * inverse
            turns = phase * (1.0 / (2.0 * math.pi))
            turns = turns - jnp.round(turns)
            sq = turns * turns
            cosine = poly(COS, sq)
            sine = poly(SIN, sq) * turns
            weight = area * (1.0 / (4.0 * math.pi)) * inverse
            single = single_scale * weight
            double = double_scale * weight * (nx * dx + ny * dy) * inverse * inverse
            at = pl.ds(i * 128, 128)
            bf = jnp.bfloat16
            mats[q, 0:pd, at] = (single * cosine).astype(bf)
            mats[q, pd : 2 * pd, at] = (double * (-cosine - phase * sine)).astype(bf)
            mats[q, 2 * pd : 3 * pd, at] = (single * sine).astype(bf)
            mats[q, 3 * pd : 4 * pd, at] = (double * (phase * cosine - sine)).astype(bf)

    left_lanes = (lane & 3) >= 2

    def sweep(s):
        for_dirs(lambda d: shell_recv(s, d).wait_recv())
        tile = lambda d: cols_in[s, d - 2]
        side_own = jnp.where(left_lanes, tile(LEFT), tile(RIGHT))
        side_up = jnp.where(left_lanes, tile(UL), tile(UR))
        side_down = jnp.where(left_lanes, tile(DL), tile(DR))
        v = {}
        for r in range(axial):
            edge = pltpu.roll(side_own, 4 * r, 1) if r else side_own
            v[r] = jnp.concatenate([mot[s, r], edge], axis=1)
        v[-1] = jnp.concatenate([rows_in[s, 0, 1], pltpu.roll(side_up, 4 * (axial - 1), 1)], axis=1)
        v[axial] = jnp.concatenate([rows_in[s, 1, 0], side_down], axis=1)
        width = circum + 128

        def across(x):
            return pltpu.roll(x, 1, 1) + pltpu.roll(x, width - 1, 1) - 4.0 * x

        moment = {}
        for r in range(-1, axial + 1):
            if r == -1:
                lap = across(v[r])[:, :circum] + rows_in[s, 0, 0] + v[0][:, :circum]
            elif r == axial:
                lap = across(v[r])[:, :circum] + rows_in[s, 1, 1] + v[axial - 1][:, :circum]
            else:
                lap = across(v[r]) + v[r - 1] + v[r + 1]
            moment[r] = kext[r + 1, :, : lap.shape[1]] * lap
        out = []
        for r in range(axial):
            bend = (
                across(moment[r])[:, :circum]
                + moment[r - 1][:, :circum]
                + moment[r + 1][:, :circum]
            )
            here, load = mot[s, r], frc[axial + r]
            bend_re, bend_im = bend[:8], bend[8:]
            v_re, v_im = here[:8], here[8:]
            sh, a, m = coef[0, r], coef[1, r], coef[2, r]
            res_re = load[:8] - (bend_re - loss_factor * bend_im + sh * v_re)
            res_im = load[8:] - (bend_im + loss_factor * bend_re + sh * v_im)
            new = jnp.concatenate(
                [v_re + res_re * a + res_im * m, v_im + res_im * a - res_re * m], axis=0
            )
            mot[s + 1, r] = new
            out.append(new)
        return out

    def round_body(rnd, _):
        b_all(rnd).wait_recv()
        total = None
        for q in range(nb // per):
            block = jnp.concatenate([gb[rnd, q * per + i] for i in range(per)], axis=1)
            term = dot(block, mats[q], ((1,), (1,)))
            total = term if total is None else total + term
        re, im = total[:8], total[8:]
        both = jnp.concatenate(
            [re - pltpu.roll(im, 2 * pd, 1), im + pltpu.roll(re, 2 * pd, 1)], axis=0
        )
        pressure = spread(both)
        press[...] = pressure
        double = spread(pltpu.roll(both, 128 - pd, 1))
        s = SWEEPS * rnd
        neumann = jnp.zeros((16, 128), f32)
        picked = None
        for part in split(mot[s].reshape(axial * 16, circum)):
            term = dot(part, onehot[...], ((1,), (0,)))
            picked = term if picked is None else picked + term
        picked = picked.reshape(axial, 16, 128)
        for r in range(axial):
            neumann = neumann + picked[r] * rowhot[r : r + 1]
        density = 0.5 * dens[...] + neumann - double
        dens[...] = density

        @pl.when(rnd < ITERS - 1)
        def _():
            ga_src[rnd + 1] = density.astype(jnp.bfloat16)
            a_start(rnd + 1)

        weighted = jnp.where(lane < pd, pressure * weight_row, 0.0)
        spots = jnp.concatenate([weighted * rowhot[r : r + 1] for r in range(axial)], axis=0)
        fluid = None
        for part in split(spots):
            term = dot(part, onehot[...], ((1,), (1,)))
            fluid = term if fluid is None else fluid + term
        fluid = fluid.reshape(axial, 16, circum)
        for r in range(axial):
            frc[axial + r] = frc[r] - fluid[r]

        for i in range(SWEEPS):
            rows = sweep(s + i)
            if i < SWEEPS - 1:
                shell_start(s + i + 1, rows)

                @pl.when(rnd < ITERS - 1)
                def _():
                    a_wait(rnd + 1)
                    b_start(rnd + 1)
            else:
                @pl.when(rnd < ITERS - 1)
                def _():
                    shell_start(s + i + 1, rows)
        return 0

    lax.fori_loop(0, ITERS, round_body, 0)

    density_out[...] = dens[...][:, :pd]
    pressure_out[...] = press[...][:, :pd]
    for r in range(axial):
        motion_out[:, r, :] = mot[STEPS, r]

    for j in range(1, nc):
        copy(pa_src, pa.at[j - 1], pan_send.at[j - 1], pan_recv.at[j - 1], me).wait_send()
    pb_all.wait_send()
    for_dirs(lambda d: stiff_copy(d).wait_send() if d in stiff_dirs else None)

    def finish_round(rnd, _):
        for j in range(1, nc):
            copy(ga_src.at[rnd], ga.at[rnd, j - 1], a_send.at[rnd, j - 1], a_recv.at[rnd, j - 1],
                 me).wait_send()
        b_all(rnd).wait_send()
        for i in range(SWEEPS):
            for_dirs(lambda d: shell_copy(SWEEPS * rnd + i, d).wait_send())
        return 0

    lax.fori_loop(0, ITERS, finish_round, 0)


def per_device(nb, nc, panels, node, hoops, density, motion, force, stiffness):
    pd = panels.shape[1]
    channels, axial, circum = motion.shape
    per = math.gcd(nb, 8)
    f32, bf16 = jnp.float32, jnp.bfloat16
    vmem = pl.BlockSpec(memory_space=pltpu.VMEM)
    smem = pl.BlockSpec(memory_space=pltpu.SMEM)
    dma = pltpu.SemaphoreType.DMA
    scratch = [
        pltpu.VMEM((STEPS + 1, axial, channels, circum), f32),
        pltpu.VMEM((2 * axial, channels, circum), f32),
        pltpu.VMEM((STEPS, 2, 2, channels, circum), f32),
        pltpu.VMEM((STEPS, 6, channels, 128), f32),
        pltpu.VMEM((STEPS, channels, 128), f32),
        pltpu.VMEM((4, axial, circum), f32),
        pltpu.VMEM((axial + 2, channels, circum + 128), f32),
        pltpu.VMEM((3, axial, 8, circum), f32),
        pltpu.VMEM((circum, 128), bf16),
        pltpu.VMEM((8, 128), f32),
        pltpu.VMEM((channels, 128), f32),
        pltpu.VMEM((channels, 128), f32),
        pltpu.VMEM((24, 128), f32),
        pltpu.VMEM((ITERS, nc - 1, channels, 128), bf16),
        pltpu.VMEM((ITERS, nb, channels, 128), bf16),
        pltpu.VMEM((ITERS, channels, 128), bf16),
        pltpu.VMEM((nc - 1, 8, 128), f32),
        pltpu.VMEM((nb, 8, 128), f32),
        pltpu.VMEM((8, 128), f32),
        pltpu.VMEM((nb // per, 4 * pd, per * 128), bf16),
        dma((STEPS, 8)), dma((STEPS, 8)), dma((4,)), dma((4,)),
        dma((ITERS, nc - 1)), dma((ITERS, nc - 1)), dma((ITERS,)), dma((ITERS,)),
        dma((nc,)), dma((nc,)),
    ]
    return pl.pallas_call(
        functools.partial(kernel, nb, nc, pd),
        out_shape=(
            jax.ShapeDtypeStruct(density.shape, f32),
            jax.ShapeDtypeStruct(density.shape, f32),
            jax.ShapeDtypeStruct(motion.shape, f32),
        ),
        in_specs=[vmem, smem, smem, vmem, vmem, vmem, vmem],
        out_specs=(vmem, vmem, vmem),
        scratch_shapes=scratch,
        compiler_params=pltpu.CompilerParams(
            collective_id=0, has_side_effects=True, vmem_limit_bytes=40 * 1024 * 1024
        ),
    )(panels, node, hoops, density, motion, force, stiffness)


def solution(mesh):
    nb, nc = mesh.shape["blk"], mesh.shape["circ"]
    in_specs = (
        P(None, ("blk", "circ")),
        P(("blk", "circ")),
        P(),
        P(None, ("blk", "circ")),
        P(None, "blk", "circ"),
        P(None, "blk", "circ"),
        P("blk", "circ"),
    )
    out_specs = (P(None, ("blk", "circ")), P(None, ("blk", "circ")), P(None, "blk", "circ"))
    return jax.shard_map(
        functools.partial(per_device, nb, nc),
        mesh=mesh, in_specs=in_specs, out_specs=out_specs, check_vma=False,
    )
```

time: 320 us -> 53.7 us (0.17)
  blocking collectives: 193 us -> 0 us
  starting transfers between devices: 60.4 us -> 0 us
  Pallas kernels: 0 us -> 45.8 us
  waiting for transfers between devices: 36.9 us -> 0 us
  other arithmetic: 16.6 us -> 0 us
  local copies, waits for them, and re-layouts: 10.9 us -> 7.04 us
    all_gather x5 -> x0, blocking collectives: 193 us -> none  [the longest x4 154 us: per_device(): lax.all_gather(density_bf, ('blk', 'circ'), axis=1, tiled=True)]
    ppermute x36 -> x0, starting transfers between devices: 60.4 us -> none  [the longest x18 55.8 us: padded(): lax.ppermute(lax.slice_in_dim(block, 0, width, axis=dim), axis, backward)]
    pallas_call x0 -> x1, Pallas kernels: none -> 45.8 us  [per_device(): pl.pallas_call(functools.partial(kernel, nb, nc, pd), out_shape=(jax.Shap...]
    ppermute x36 -> x0, waiting for transfers between devices: 36.9 us -> none  [the longest x18 36.8 us: padded(): lax.ppermute(lax.slice_in_dim(block, block.shape[dim] - width, None, axis...]
    select_n x17 -> x0, other arithmetic: 6.29 us -> none  [the longest x16 6.28 us: clear_outside(): return jnp.where(inside[:, None], extended, 0.0)]
    unnamed x20 -> x17, local copies, waits for them, and re-layouts: 2.77 us -> 7.04 us
    scatter-add x4 -> x0, other arithmetic: 3.86 us -> none  [per_device(): fluid = fluid.at[:, node_of_panel].add(panel_weight[None, :] * pressure)]
  transfers between devices with their start and end apart: 36 -> 0, of which waited for: 13 -> 0; matrix products, arithmetic and copies ran while one was open for 4% -> 0% of each run, Pallas kernels for 0% -> 0%
where the time goes in v1:
time: 53.7 us; the launch traced here: 53.4 us
  Pallas kernels  45.8 us (85%)
  local copies, waits for them, and re-layouts  7.04 us (13%)
  between operations  0.66 us (1%)
    pallas_call x1, Pallas kernels, per_device(): pl.pallas_call(functools.partial(kernel, nb, nc, pd), out_shape=(jax.Shap...  45.8 us
    unnamed x17, local copies, waits for them, and re-layouts  7.04 us

profile of v1, /device:TPU:0, one launch (start us, length us, event | category | flops | bytes accessed | tf_op | source)
XLA Modules:
  0.0 53.4 jit_solution(5504959645978542494)
XLA Ops:
  0.6 0.0 copy-start
  0.6 0.9 %copy-done = f32[16,8,256]{2,1,0:T(8,128)S(1)} copy-done((f32[16,8,256]{2,1,0:T(8,128)S(1)}, f32[16,8,256]{2,1,0:T(8,128)}, u32[]{:S(2)}) %copy-start) | copy-done | bytes 131096
  1.5 0.0 copy-start.1
  1.5 0.9 %copy-done.1 = f32[16,8,256]{2,1,0:T(8,128)S(1)} copy-done((f32[16,8,256]{2,1,0:T(8,128)S(1)}, f32[16,8,256]{2,1,0:T(8,128)}, u32[]{:S(2)}) %copy-start.1) | copy-done | bytes 131096
  2.4 0.0 copy-start.2
  2.4 0.7 %copy-done.2 = f32[16,32]{1,0:T(8,128)S(1)} copy-done((f32[16,32]{1,0:T(8,128)S(1)}, f32[16,32]{1,0:T(8,128)}, u32[]{:S(2)}) %copy-start.2) | copy-done | bytes 2072
  3.1 0.0 copy-start.3
  3.1 0.7 %copy-done.3 = f32[8,256]{1,0:T(8,128)S(1)} copy-done((f32[8,256]{1,0:T(8,128)S(1)}, f32[8,256]{1,0:T(8,128)}, u32[]{:S(2)}) %copy-start.3) | copy-done | bytes 8216
  3.8 0.0 copy-start.4
  3.8 0.7 %copy-done.4 = f32[4,32]{1,0:T(4,128)S(1)} copy-done((f32[4,32]{1,0:T(4,128)S(1)}, f32[4,32]{1,0:T(4,128)}, u32[]{:S(2)}) %copy-start.4) | copy-done | bytes 536
  4.5 0.0 copy-start.5
  4.5 0.7 %copy-done.5 = s32[32]{0:T(128)S(1)} copy-done((s32[32]{0:T(128)S(1)}, s32[32]{0:T(128)}, u32[]{:S(2)}) %copy-start.5) | copy-done | bytes 152
  5.2 0.0 copy-start.6
  5.2 0.7 %copy-done.6 = s32[4]{0:T(128)S(1)} copy-done((s32[4]{0:T(128)S(1)}, s32[4]{0:T(128)}, u32[]{:S(2)}) %copy-start.6) | copy-done | bytes 40
  5.8 45.8 %shard_map.94 = (f32[16,32]{1,0:T(8,128)S(1)}, f32[16,32]{1,0:T(8,128)S(1)}, f32[16,8,256]{2,1,0:T(8,128)S(1)}) custom-call(f32[4,32]{1,0:T(4,128)S(1)} %copy-done.4, s32[32]{0:T(128)S(1)} %copy-done.5, s32[4]{0:T(128)S(1)} %copy-done.6, f32[16,32]{1,0:T(8,128)S(1)} %copy-done.2, f32[16,8,256]{2,1,0:T(8,128)S(1)} %copy-done, f32[16,8,256]{2,1,0:T(8,128)S(1)} %copy-done.1, ...), custom_call_target="tpu_custom_call" | custom-call | tf_op jit(solution)/shard_map/pallas_call | solution.py:492
  51.6 0.6 %copy.13 = f32[16,32]{1,0:T(8,128)} copy(f32[16,32]{1,0:T(8,128)S(1)} %get-tuple-element.6) | data formatting | bytes 4096
  52.2 0.6 %copy.14 = f32[16,32]{1,0:T(8,128)} copy(f32[16,32]{1,0:T(8,128)S(1)} %get-tuple-element.7) | data formatting | bytes 4096
  52.8 0.7 %copy.15 = f32[16,8,256]{2,1,0:T(8,128)} copy(f32[16,8,256]{2,1,0:T(8,128)S(1)} %get-tuple-element.8) | data formatting | bytes 262144
Async XLA Ops:
  0.6 0.9 %copy-start = (f32[16,8,256]{2,1,0:T(8,128)S(1)}, f32[16,8,256]{2,1,0:T(8,128)}, u32[]{:S(2)}) copy-start(f32[16,8,256]{2,1,0:T(8,128)} %motion_in.1) | copy-start | bytes 393220
  1.5 0.9 %copy-start.1 = (f32[16,8,256]{2,1,0:T(8,128)S(1)}, f32[16,8,256]{2,1,0:T(8,128)}, u32[]{:S(2)}) copy-start(f32[16,8,256]{2,1,0:T(8,128)} %force_in.1) | copy-start | bytes 393220
  2.4 0.7 %copy-start.2 = (f32[16,32]{1,0:T(8,128)S(1)}, f32[16,32]{1,0:T(8,128)}, u32[]{:S(2)}) copy-start(f32[16,32]{1,0:T(8,128)} %density_in.1) | copy-start | bytes 6148
  3.1 0.7 %copy-start.3 = (f32[8,256]{1,0:T(8,128)S(1)}, f32[8,256]{1,0:T(8,128)}, u32[]{:S(2)}) copy-start(f32[8,256]{1,0:T(8,128)} %stiff.1) | copy-start | bytes 24580
  3.8 0.7 %copy-start.4 = (f32[4,32]{1,0:T(4,128)S(1)}, f32[4,32]{1,0:T(4,128)}, u32[]{:S(2)}) copy-start(f32[4,32]{1,0:T(4,128)} %panels.1) | copy-start | bytes 1540
  4.5 0.7 %copy-start.5 = (s32[32]{0:T(128)S(1)}, s32[32]{0:T(128)}, u32[]{:S(2)}) copy-start(s32[32]{0:T(128)} %node.1) | copy-start | bytes 388
  5.2 0.7 %copy-start.6 = (s32[4]{0:T(128)S(1)}, s32[4]{0:T(128)}, u32[]{:S(2)}) copy-start(s32[4]{0:T(128)} %hoops.1) | copy-start | bytes 52

commit v2 on v1

--- a/solution.py
+++ b/solution.py
@@ -53,11 +53,12 @@
 
 def kernel(
     nb, nc, pd,
-    panels, node, hoops, density_in, motion_in, force_in, stiff,
+    panels_hbm, node_hbm, hoops_hbm, density_hbm, motion_hbm, force_hbm, stiff_hbm,
     density_out, pressure_out, motion_out,
     mot, frc, rows_in, cols_in, cols_own, stiff_in, kext, coef, onehot, rowhot,
     dens, press, wide, ga, gb, ga_src, pa, pb, pa_src, mats,
     sh_send, sh_recv, st_send, st_recv, a_send, a_recv, b_send, b_recv, pan_send, pan_recv,
+    panels, node, hoops, density_in, motion_in, force_in, stiff, in_sems,
 ):
     f32 = jnp.float32
     b = lax.axis_index("blk")
@@ -96,6 +97,16 @@
 
             lax.fori_loop(1, nb, body, 0)
 
+    loads = [
+        pltpu.make_async_copy(src, dst, in_sems.at[n])
+        for n, (src, dst) in enumerate((
+            (panels_hbm, panels), (density_hbm, density_in), (motion_hbm, motion_in),
+            (stiff_hbm, stiff), (force_hbm, force_in), (node_hbm, node), (hoops_hbm, hoops),
+        ))
+    ]
+    for load in loads:
+        load.start()
+
     @pl.when(jnp.logical_not(has_up))
     def _():
         rows_in[:, 0] = jnp.zeros_like(rows_in[:, 0])
@@ -141,6 +152,8 @@
         return x
 
     wide[...] = jnp.zeros_like(wide)
+    loads[0].wait()
+    loads[1].wait()
     wide[0:4, 0:pd] = panels[...]
     wide[8:24, 0:pd] = density_in[...]
     own = spread(wide[0:8, :])
@@ -192,6 +205,7 @@
         copy(pa_src, pa.at[j - 1], pan_send.at[j - 1], pan_recv.at[j - 1],
              (b, lax.rem(c + j, nc))).start()
     a_start(0)
+    loads[3].wait()
     stiff_dirs = (UP, DOWN, LEFT, RIGHT)
 
     def stiff_copy(d):
@@ -228,12 +242,15 @@
         cols_own[s] = packed
         for_dirs(lambda d: shell_copy(s, d).start())
 
+    loads[2].wait()
     first = []
     for r in range(axial):
         row = motion_in[:, r, :]
         mot[0, r] = row
         first.append(row)
     shell_start(0, first)
+    for load in loads[4:]:
+        load.wait()
     for r in range(axial):
         frc[r] = force_in[:, r, :]
 
@@ -462,7 +479,7 @@
     per = math.gcd(nb, 8)
     f32, bf16 = jnp.float32, jnp.bfloat16
     vmem = pl.BlockSpec(memory_space=pltpu.VMEM)
-    smem = pl.BlockSpec(memory_space=pltpu.SMEM)
+    hbm = pl.BlockSpec(memory_space=pltpu.HBM)
     dma = pltpu.SemaphoreType.DMA
     scratch = [
         pltpu.VMEM((STEPS + 1, axial, channels, circum), f32),
@@ -488,6 +505,10 @@
         dma((STEPS, 8)), dma((STEPS, 8)), dma((4,)), dma((4,)),
         dma((ITERS, nc - 1)), dma((ITERS, nc - 1)), dma((ITERS,)), dma((ITERS,)),
         dma((nc,)), dma((nc,)),
+        pltpu.VMEM(panels.shape, f32), pltpu.SMEM(node.shape, jnp.int32),
+        pltpu.SMEM(hoops.shape, jnp.int32), pltpu.VMEM(density.shape, f32),
+        pltpu.VMEM(motion.shape, f32), pltpu.VMEM(force.shape, f32),
+        pltpu.VMEM(stiffness.shape, f32), dma((7,)),
     ]
     return pl.pallas_call(
         functools.partial(kernel, nb, nc, pd),
@@ -496,11 +517,11 @@
             jax.ShapeDtypeStruct(density.shape, f32),
             jax.ShapeDtypeStruct(motion.shape, f32),
         ),
-        in_specs=[vmem, smem, smem, vmem, vmem, vmem, vmem],
+        in_specs=[hbm] * 7,
         out_specs=(vmem, vmem, vmem),
         scratch_shapes=scratch,
         compiler_params=pltpu.CompilerParams(
-            collective_id=0, has_side_effects=True, vmem_limit_bytes=40 * 1024 * 1024
+            collective_id=0, has_side_effects=True, vmem_limit_bytes=64 * 1024 * 1024
         ),
     )(panels, node, hoops, density, motion, force, stiffness)
 

time: 53.7 us -> 50.3 us (0.937)
  local copies, waits for them, and re-layouts: 7.04 us -> 3.47 us
    unnamed x17 -> x5, local copies, waits for them, and re-layouts: 7.04 us -> 3.47 us
where the time goes in v2:
time: 50.3 us; the launch traced here: 50 us
  Pallas kernels  45.9 us (91%)
  local copies, waits for them, and re-layouts  3.47 us (7%)
  between operations  0.65 us (1%)
    pallas_call x1, Pallas kernels, per_device(): pl.pallas_call(functools.partial(kernel, nb, nc, pd), out_shape=(jax.Shap...  45.9 us
    unnamed x5, local copies, waits for them, and re-layouts  3.47 us

profile of v2, /device:TPU:0, one launch (start us, length us, event | category | flops | bytes accessed | tf_op | source)
XLA Modules:
  0.0 50.0 jit_solution(11787327858934610532)
XLA Ops:
  0.6 45.9 %shard_map.94 = (f32[16,32]{1,0:T(8,128)}, f32[16,32]{1,0:T(8,128)}, f32[16,8,256]{2,1,0:T(8,128)}) custom-call(f32[4,32]{1,0:T(4,128)} %panels_hbm.1, s32[32]{0:T(128)} %node_hbm.1, s32[4]{0:T(128)} %hoops_hbm.1, f32[16,32]{1,0:T(8,128)} %density_hbm.1, f32[16,8,256]{2,1,0:T(8,128)} %motion_hbm.1, f32[16,8,256]{2,1,0:T(8,128)} %force_hbm.1, f32[8,256]{1,0:T(8,128)} %stiff_hbm.1), custom_call_target="tpu_custom_call" | custom-call | tf_op jit(solution)/shard_map/pallas_call | solution.py:513
  46.6 0.0 copy-start
  46.6 1.3 %copy.13 = f32[16,32]{1,0:T(8,128)} copy(f32[16,32]{1,0:T(8,128)} %get-tuple-element.6) | data formatting | bytes 4096
  47.9 0.0 copy-done
  47.9 0.6 %copy.14 = f32[16,32]{1,0:T(8,128)} copy(f32[16,32]{1,0:T(8,128)S(1)} %copy-done) | data formatting | bytes 4096
  48.5 1.6 %copy.15 = f32[16,8,256]{2,1,0:T(8,128)} copy(f32[16,8,256]{2,1,0:T(8,128)} %get-tuple-element.8) | data formatting | bytes 262144
Async XLA Ops:
  46.6 1.3 %copy-start = (f32[16,32]{1,0:T(8,128)S(1)}, f32[16,32]{1,0:T(8,128)}, u32[]{:S(2)}) copy-start(f32[16,32]{1,0:T(8,128)} %get-tuple-element.7) | copy-start | bytes 6148

commit v3 on v2

--- a/solution.py
+++ b/solution.py
@@ -55,7 +55,7 @@
     nb, nc, pd,
     panels_hbm, node_hbm, hoops_hbm, density_hbm, motion_hbm, force_hbm, stiff_hbm,
     density_out, pressure_out, motion_out,
-    mot, frc, rows_in, cols_in, cols_own, stiff_in, kext, coef, onehot, rowhot,
+    mot, frc, rows_own, rows_in, cols_in, cols_own, stiff_in, kext, coef, onehot, rowhot,
     dens, press, wide, ga, gb, ga_src, pa, pb, pa_src, mats,
     sh_send, sh_recv, st_send, st_recv, a_send, a_recv, b_send, b_recv, pan_send, pan_recv,
     panels, node, hoops, density_in, motion_in, force_in, stiff, in_sems,
@@ -73,9 +73,6 @@
     has_up, has_down = b > 0, b < nb - 1
 
     def for_dirs(fn):
-        fn(LEFT)
-        fn(RIGHT)
-
         @pl.when(has_up)
         def _():
             for d in (UP, UL, UR):
@@ -85,6 +82,9 @@
         def _():
             for d in (DOWN, DL, DR):
                 fn(d)
+
+        fn(LEFT)
+        fn(RIGHT)
 
     def for_peers(fn):
         if nb <= 8:
@@ -217,7 +217,7 @@
     def shell_copy(s, d):
         o = OPPOSITE[d]
         if d in (UP, DOWN):
-            src = mot.at[s, pl.ds(0 if d == UP else axial - 2, 2)]
+            src = rows_own.at[s, 0 if d == UP else 1]
             dst = rows_in.at[s, 0 if o == UP else 1]
         else:
             src, dst = cols_own.at[s], cols_in.at[s, o - 2]
@@ -239,7 +239,11 @@
             edge = jnp.where(lane < 64, rows[r][:, :128], rows[r][:, last_tile:])
             edge = pltpu.roll(edge, (128 - 4 * r) % 128, 1) if r else edge
             packed = edge if r == 0 else jnp.where(row_of == r, edge, packed)
-        cols_own[s] = packed
+        bf = jnp.bfloat16
+        cols_own[s] = packed.astype(bf)
+        for n, at in enumerate((0, axial - 2)):
+            for i in range(2):
+                rows_own[s, n, i] = rows[at + i].astype(bf)
         for_dirs(lambda d: shell_copy(s, d).start())
 
     loads[2].wait()
@@ -349,16 +353,18 @@
 
     def sweep(s):
         for_dirs(lambda d: shell_recv(s, d).wait_recv())
-        tile = lambda d: cols_in[s, d - 2]
+        tile = lambda d: cols_in[s, d - 2].astype(f32)
         side_own = jnp.where(left_lanes, tile(LEFT), tile(RIGHT))
         side_up = jnp.where(left_lanes, tile(UL), tile(UR))
         side_down = jnp.where(left_lanes, tile(DL), tile(DR))
+        above = [rows_in[s, 0, i].astype(f32) for i in range(2)]
+        below = [rows_in[s, 1, i].astype(f32) for i in range(2)]
         v = {}
         for r in range(axial):
             edge = pltpu.roll(side_own, 4 * r, 1) if r else side_own
             v[r] = jnp.concatenate([mot[s, r], edge], axis=1)
-        v[-1] = jnp.concatenate([rows_in[s, 0, 1], pltpu.roll(side_up, 4 * (axial - 1), 1)], axis=1)
-        v[axial] = jnp.concatenate([rows_in[s, 1, 0], side_down], axis=1)
+        v[-1] = jnp.concatenate([above[1], pltpu.roll(side_up, 4 * (axial - 1), 1)], axis=1)
+        v[axial] = jnp.concatenate([below[0], side_down], axis=1)
         width = circum + 128
 
         def across(x):
@@ -367,9 +373,9 @@
         moment = {}
         for r in range(-1, axial + 1):
             if r == -1:
-                lap = across(v[r])[:, :circum] + rows_in[s, 0, 0] + v[0][:, :circum]
+                lap = across(v[r])[:, :circum] + above[0] + v[0][:, :circum]
             elif r == axial:
-                lap = across(v[r])[:, :circum] + rows_in[s, 1, 1] + v[axial - 1][:, :circum]
+                lap = across(v[r])[:, :circum] + below[1] + v[axial - 1][:, :circum]
             else:
                 lap = across(v[r]) + v[r - 1] + v[r + 1]
             moment[r] = kext[r + 1, :, : lap.shape[1]] * lap
@@ -484,9 +490,10 @@
     scratch = [
         pltpu.VMEM((STEPS + 1, axial, channels, circum), f32),
         pltpu.VMEM((2 * axial, channels, circum), f32),
-        pltpu.VMEM((STEPS, 2, 2, channels, circum), f32),
-        pltpu.VMEM((STEPS, 6, channels, 128), f32),
-        pltpu.VMEM((STEPS, channels, 128), f32),
+        pltpu.VMEM((STEPS, 2, 2, channels, circum), bf16),
+        pltpu.VMEM((STEPS, 2, 2, channels, circum), bf16),
+        pltpu.VMEM((STEPS, 6, channels, 128), bf16),
+        pltpu.VMEM((STEPS, channels, 128), bf16),
         pltpu.VMEM((4, axial, circum), f32),
         pltpu.VMEM((axial + 2, channels, circum + 128), f32),
         pltpu.VMEM((3, axial, 8, circum), f32),

time: 50.3 us -> 46.1 us (0.917)
  Pallas kernels: 45.9 us -> 41.8 us
    pallas_call x1, Pallas kernels: 45.9 us -> 41.8 us  [per_device(): pl.pallas_call(functools.partial(kernel, nb, nc, pd), out_shape=(jax.Shap...]
where the time goes in v3:
time: 46.1 us; the launch traced here: 45.9 us
  Pallas kernels  41.8 us (91%)
  local copies, waits for them, and re-layouts  3.47 us (8%)
  between operations  0.65 us (1%)
    pallas_call x1, Pallas kernels, per_device(): pl.pallas_call(functools.partial(kernel, nb, nc, pd), out_shape=(jax.Shap...  41.8 us
    unnamed x5, local copies, waits for them, and re-layouts  3.47 us

profile of v3, /device:TPU:0, one launch (start us, length us, event | category | flops | bytes accessed | tf_op | source)
XLA Modules:
  0.0 45.9 jit_solution(3902854467694721266)
XLA Ops:
  0.6 41.8 %shard_map.94 = (f32[16,32]{1,0:T(8,128)}, f32[16,32]{1,0:T(8,128)}, f32[16,8,256]{2,1,0:T(8,128)}) custom-call(f32[4,32]{1,0:T(4,128)} %panels_hbm.1, s32[32]{0:T(128)} %node_hbm.1, s32[4]{0:T(128)} %hoops_hbm.1, f32[16,32]{1,0:T(8,128)} %density_hbm.1, f32[16,8,256]{2,1,0:T(8,128)} %motion_hbm.1, f32[16,8,256]{2,1,0:T(8,128)} %force_hbm.1, f32[8,256]{1,0:T(8,128)} %stiff_hbm.1), custom_call_target="tpu_custom_call" | custom-call | tf_op jit(solution)/shard_map/pallas_call | solution.py:520
  42.4 0.0 copy-start
  42.4 1.3 %copy.13 = f32[16,32]{1,0:T(8,128)} copy(f32[16,32]{1,0:T(8,128)} %get-tuple-element.6) | data formatting | bytes 4096
  43.7 0.0 copy-done
  43.7 0.6 %copy.14 = f32[16,32]{1,0:T(8,128)} copy(f32[16,32]{1,0:T(8,128)S(1)} %copy-done) | data formatting | bytes 4096
  44.3 1.6 %copy.15 = f32[16,8,256]{2,1,0:T(8,128)} copy(f32[16,8,256]{2,1,0:T(8,128)} %get-tuple-element.8) | data formatting | bytes 262144
Async XLA Ops:
  42.4 1.3 %copy-start = (f32[16,32]{1,0:T(8,128)S(1)}, f32[16,32]{1,0:T(8,128)}, u32[]{:S(2)}) copy-start(f32[16,32]{1,0:T(8,128)} %get-tuple-element.7) | copy-start | bytes 6148

commit v4 on v3

--- a/solution.py
+++ b/solution.py
@@ -443,12 +443,12 @@
         for i in range(SWEEPS):
             rows = sweep(s + i)
             if i < SWEEPS - 1:
-                shell_start(s + i + 1, rows)
-
                 @pl.when(rnd < ITERS - 1)
                 def _():
                     a_wait(rnd + 1)
                     b_start(rnd + 1)
+
+                shell_start(s + i + 1, rows)
             else:
                 @pl.when(rnd < ITERS - 1)
                 def _():

time: 46.1 us -> 48.8 us (1.059)
  Pallas kernels: 41.8 us -> 44.5 us
    pallas_call x1, Pallas kernels: 41.8 us -> 44.5 us  [per_device(): pl.pallas_call(functools.partial(kernel, nb, nc, pd), out_shape=(jax.Shap...]
where the time goes in v4:
time: 48.8 us; the launch traced here: 48.6 us
  Pallas kernels  44.5 us (91%)
  local copies, waits for them, and re-layouts  3.47 us (7%)
  between operations  0.65 us (1%)
    pallas_call x1, Pallas kernels, per_device(): pl.pallas_call(functools.partial(kernel, nb, nc, pd), out_shape=(jax.Shap...  44.5 us
    unnamed x5, local copies, waits for them, and re-layouts  3.47 us

profile of v4, /device:TPU:0, one launch (start us, length us, event | category | flops | bytes accessed | tf_op | source)
XLA Modules:
  0.0 48.6 jit_solution(2770488151158912104)
XLA Ops:
  0.6 44.5 %shard_map.94 = (f32[16,32]{1,0:T(8,128)}, f32[16,32]{1,0:T(8,128)}, f32[16,8,256]{2,1,0:T(8,128)}) custom-call(f32[4,32]{1,0:T(4,128)} %panels_hbm.1, s32[32]{0:T(128)} %node_hbm.1, s32[4]{0:T(128)} %hoops_hbm.1, f32[16,32]{1,0:T(8,128)} %density_hbm.1, f32[16,8,256]{2,1,0:T(8,128)} %motion_hbm.1, f32[16,8,256]{2,1,0:T(8,128)} %force_hbm.1, f32[8,256]{1,0:T(8,128)} %stiff_hbm.1), custom_call_target="tpu_custom_call" | custom-call | tf_op jit(solution)/shard_map/pallas_call | solution.py:520
  45.1 0.0 copy-start
  45.1 1.3 %copy.13 = f32[16,32]{1,0:T(8,128)} copy(f32[16,32]{1,0:T(8,128)} %get-tuple-element.6) | data formatting | bytes 4096
  46.4 0.0 copy-done
  46.4 0.6 %copy.14 = f32[16,32]{1,0:T(8,128)} copy(f32[16,32]{1,0:T(8,128)S(1)} %copy-done) | data formatting | bytes 4096
  47.0 1.6 %copy.15 = f32[16,8,256]{2,1,0:T(8,128)} copy(f32[16,8,256]{2,1,0:T(8,128)} %get-tuple-element.8) | data formatting | bytes 262144
Async XLA Ops:
  45.1 1.3 %copy-start = (f32[16,32]{1,0:T(8,128)S(1)}, f32[16,32]{1,0:T(8,128)}, u32[]{:S(2)}) copy-start(f32[16,32]{1,0:T(8,128)} %get-tuple-element.7) | copy-start | bytes 6148

commit v5 on v3

--- a/solution.py
+++ b/solution.py
@@ -72,7 +72,7 @@
     }
     has_up, has_down = b > 0, b < nb - 1
 
-    def for_dirs(fn):
+    def for_far(fn):
         @pl.when(has_up)
         def _():
             for d in (UP, UL, UR):
@@ -83,6 +83,8 @@
             for d in (DOWN, DL, DR):
                 fn(d)
 
+    def for_dirs(fn):
+        for_far(fn)
         fn(LEFT)
         fn(RIGHT)
 
@@ -352,35 +354,17 @@
     left_lanes = (lane & 3) >= 2
 
     def sweep(s):
-        for_dirs(lambda d: shell_recv(s, d).wait_recv())
         tile = lambda d: cols_in[s, d - 2].astype(f32)
-        side_own = jnp.where(left_lanes, tile(LEFT), tile(RIGHT))
-        side_up = jnp.where(left_lanes, tile(UL), tile(UR))
-        side_down = jnp.where(left_lanes, tile(DL), tile(DR))
-        above = [rows_in[s, 0, i].astype(f32) for i in range(2)]
-        below = [rows_in[s, 1, i].astype(f32) for i in range(2)]
-        v = {}
-        for r in range(axial):
-            edge = pltpu.roll(side_own, 4 * r, 1) if r else side_own
-            v[r] = jnp.concatenate([mot[s, r], edge], axis=1)
-        v[-1] = jnp.concatenate([above[1], pltpu.roll(side_up, 4 * (axial - 1), 1)], axis=1)
-        v[axial] = jnp.concatenate([below[0], side_down], axis=1)
         width = circum + 128
+        v, moment, out = {}, {}, {}
 
         def across(x):
             return pltpu.roll(x, 1, 1) + pltpu.roll(x, width - 1, 1) - 4.0 * x
 
-        moment = {}
-        for r in range(-1, axial + 1):
-            if r == -1:
-                lap = across(v[r])[:, :circum] + above[0] + v[0][:, :circum]
-            elif r == axial:
-                lap = across(v[r])[:, :circum] + below[1] + v[axial - 1][:, :circum]
-            else:
-                lap = across(v[r]) + v[r - 1] + v[r + 1]
+        def bending(r, lap):
             moment[r] = kext[r + 1, :, : lap.shape[1]] * lap
-        out = []
-        for r in range(axial):
+
+        def update(r):
             bend = (
                 across(moment[r])[:, :circum]
                 + moment[r - 1][:, :circum]
@@ -396,8 +380,33 @@
                 [v_re + res_re * a + res_im * m, v_im + res_im * a - res_re * m], axis=0
             )
             mot[s + 1, r] = new
-            out.append(new)
-        return out
+            out[r] = new
+
+        shell_recv(s, LEFT).wait_recv()
+        shell_recv(s, RIGHT).wait_recv()
+        side_own = jnp.where(left_lanes, tile(LEFT), tile(RIGHT))
+        for r in range(axial):
+            edge = pltpu.roll(side_own, 4 * r, 1) if r else side_own
+            v[r] = jnp.concatenate([mot[s, r], edge], axis=1)
+        for r in range(1, axial - 1):
+            bending(r, across(v[r]) + v[r - 1] + v[r + 1])
+        for r in range(2, axial - 2):
+            update(r)
+
+        for_far(lambda d: shell_recv(s, d).wait_recv())
+        side_up = jnp.where(left_lanes, tile(UL), tile(UR))
+        side_down = jnp.where(left_lanes, tile(DL), tile(DR))
+        above = [rows_in[s, 0, i].astype(f32) for i in range(2)]
+        below = [rows_in[s, 1, i].astype(f32) for i in range(2)]
+        v[-1] = jnp.concatenate([above[1], pltpu.roll(side_up, 4 * (axial - 1), 1)], axis=1)
+        v[axial] = jnp.concatenate([below[0], side_down], axis=1)
+        bending(-1, across(v[-1])[:, :circum] + above[0] + v[0][:, :circum])
+        bending(axial, across(v[axial])[:, :circum] + below[1] + v[axial - 1][:, :circum])
+        for r in (0, axial - 1):
+            bending(r, across(v[r]) + v[r - 1] + v[r + 1])
+        for r in (0, 1, axial - 2, axial - 1):
+            update(r)
+        return [out[r] for r in range(axial)]
 
     def round_body(rnd, _):
         b_all(rnd).wait_recv()

time: 46.1 us -> 45.7 us (level)
  Pallas kernels: 41.8 us -> 41.3 us
where the time goes in v5:
time: 45.7 us; the launch traced here: 45.4 us
  Pallas kernels  41.3 us (90%)
  local copies, waits for them, and re-layouts  3.47 us (8%)
  between operations  0.65 us (1%)
    pallas_call x1, Pallas kernels, per_device(): pl.pallas_call(functools.partial(kernel, nb, nc, pd), out_shape=(jax.Shap...  41.3 us
    unnamed x5, local copies, waits for them, and re-layouts  3.47 us

profile of v5, /device:TPU:0, one launch (start us, length us, event | category | flops | bytes accessed | tf_op | source)
XLA Modules:
  0.0 45.4 jit_solution(14197889102369822805)
XLA Ops:
  0.6 41.3 %shard_map.94 = (f32[16,32]{1,0:T(8,128)}, f32[16,32]{1,0:T(8,128)}, f32[16,8,256]{2,1,0:T(8,128)}) custom-call(f32[4,32]{1,0:T(4,128)} %panels_hbm.1, s32[32]{0:T(128)} %node_hbm.1, s32[4]{0:T(128)} %hoops_hbm.1, f32[16,32]{1,0:T(8,128)} %density_hbm.1, f32[16,8,256]{2,1,0:T(8,128)} %motion_hbm.1, f32[16,8,256]{2,1,0:T(8,128)} %force_hbm.1, f32[8,256]{1,0:T(8,128)} %stiff_hbm.1), custom_call_target="tpu_custom_call" | custom-call | tf_op jit(solution)/shard_map/pallas_call | solution.py:529
  42.0 0.0 copy-start
  42.0 1.3 %copy.13 = f32[16,32]{1,0:T(8,128)} copy(f32[16,32]{1,0:T(8,128)} %get-tuple-element.6) | data formatting | bytes 4096
  43.3 0.0 copy-done
  43.3 0.6 %copy.14 = f32[16,32]{1,0:T(8,128)} copy(f32[16,32]{1,0:T(8,128)S(1)} %copy-done) | data formatting | bytes 4096
  43.9 1.6 %copy.15 = f32[16,8,256]{2,1,0:T(8,128)} copy(f32[16,8,256]{2,1,0:T(8,128)} %get-tuple-element.8) | data formatting | bytes 262144
Async XLA Ops:
  42.0 1.3 %copy-start = (f32[16,32]{1,0:T(8,128)S(1)}, f32[16,32]{1,0:T(8,128)}, u32[]{:S(2)}) copy-start(f32[16,32]{1,0:T(8,128)} %get-tuple-element.7) | copy-start | bytes 6148

commit v6 on v5

--- a/solution.py
+++ b/solution.py
@@ -56,7 +56,7 @@
     panels_hbm, node_hbm, hoops_hbm, density_hbm, motion_hbm, force_hbm, stiff_hbm,
     density_out, pressure_out, motion_out,
     mot, frc, rows_own, rows_in, cols_in, cols_own, stiff_in, kext, coef, onehot, rowhot,
-    dens, press, wide, ga, gb, ga_src, pa, pb, pa_src, mats,
+    dens, held, press, wide, ga, gb, ga_src, pa, pb, pa_src, mats,
     sh_send, sh_recv, st_send, st_recv, a_send, a_recv, b_send, b_recv, pan_send, pan_recv,
     panels, node, hoops, density_in, motion_in, force_in, stiff, in_sems,
 ):
@@ -313,6 +313,17 @@
             kext[r, :, circum:] = jnp.broadcast_to(side[r - 1 : r], (16, 128))
         kext[r, :, :circum] = jnp.broadcast_to(line, (16, circum))
 
+    def hold(s):
+        neumann = jnp.zeros((16, 128), f32)
+        picked = None
+        for part in split(mot[s].reshape(axial * 16, circum)):
+            term = dot(part, onehot[...], ((1,), (0,)))
+            picked = term if picked is None else picked + term
+        picked = picked.reshape(axial, 16, 128)
+        for r in range(axial):
+            neumann = neumann + picked[r] * rowhot[r : r + 1]
+        held[...] = 0.5 * dens[...] + neumann
+
     radial = jnp.sqrt(own[0:1] * own[0:1] + own[1:2] * own[1:2])
     eye = lax.broadcasted_iota(jnp.int32, (pd, 128), 0) == lax.broadcasted_iota(
         jnp.int32, (pd, 128), 1
@@ -325,6 +336,7 @@
     nx, ny = column(own[0:1] / radial), column(own[1:2] / radial)
     weight_row = own[3:4] * (pd * nb * nc / (8.0 * math.pi))
 
+    hold(0)
     pb_all.wait_recv()
 
     per = mats.shape[2] // 128
@@ -423,15 +435,7 @@
         press[...] = pressure
         double = spread(pltpu.roll(both, 128 - pd, 1))
         s = SWEEPS * rnd
-        neumann = jnp.zeros((16, 128), f32)
-        picked = None
-        for part in split(mot[s].reshape(axial * 16, circum)):
-            term = dot(part, onehot[...], ((1,), (0,)))
-            picked = term if picked is None else picked + term
-        picked = picked.reshape(axial, 16, 128)
-        for r in range(axial):
-            neumann = neumann + picked[r] * rowhot[r : r + 1]
-        density = 0.5 * dens[...] + neumann - double
+        density = held[...] - double
         dens[...] = density
 
         @pl.when(rnd < ITERS - 1)
@@ -462,6 +466,7 @@
                 @pl.when(rnd < ITERS - 1)
                 def _():
                     shell_start(s + i + 1, rows)
+                    hold(s + i + 1)
         return 0
 
     lax.fori_loop(0, ITERS, round_body, 0)
@@ -508,6 +513,7 @@
         pltpu.VMEM((3, axial, 8, circum), f32),
         pltpu.VMEM((circum, 128), bf16),
         pltpu.VMEM((8, 128), f32),
+        pltpu.VMEM((channels, 128), f32),
         pltpu.VMEM((channels, 128), f32),
         pltpu.VMEM((channels, 128), f32),
         pltpu.VMEM((24, 128), f32),

time: 45.7 us -> 45.6 us (level)
  no operation moved by 1% of the time
where the time goes in v6:
time: 45.6 us; the launch traced here: 45.4 us
  Pallas kernels  41.3 us (91%)
  local copies, waits for them, and re-layouts  3.47 us (8%)
  between operations  0.65 us (1%)
    pallas_call x1, Pallas kernels, per_device(): pl.pallas_call(functools.partial(kernel, nb, nc, pd), out_shape=(jax.Shap...  41.3 us
    unnamed x5, local copies, waits for them, and re-layouts  3.47 us

profile of v6, /device:TPU:0, one launch (start us, length us, event | category | flops | bytes accessed | tf_op | source)
XLA Modules:
  0.0 45.4 jit_solution(1364867348708679216)
XLA Ops:
  0.6 41.3 %shard_map.94 = (f32[16,32]{1,0:T(8,128)}, f32[16,32]{1,0:T(8,128)}, f32[16,8,256]{2,1,0:T(8,128)}) custom-call(f32[4,32]{1,0:T(4,128)} %panels_hbm.1, s32[32]{0:T(128)} %node_hbm.1, s32[4]{0:T(128)} %hoops_hbm.1, f32[16,32]{1,0:T(8,128)} %density_hbm.1, f32[16,8,256]{2,1,0:T(8,128)} %motion_hbm.1, f32[16,8,256]{2,1,0:T(8,128)} %force_hbm.1, f32[8,256]{1,0:T(8,128)} %stiff_hbm.1), custom_call_target="tpu_custom_call" | custom-call | tf_op jit(solution)/shard_map/pallas_call | solution.py:535
  41.9 0.0 copy-start
  41.9 1.3 %copy.13 = f32[16,32]{1,0:T(8,128)} copy(f32[16,32]{1,0:T(8,128)} %get-tuple-element.6) | data formatting | bytes 4096
  43.2 0.0 copy-done
  43.2 0.6 %copy.14 = f32[16,32]{1,0:T(8,128)} copy(f32[16,32]{1,0:T(8,128)S(1)} %copy-done) | data formatting | bytes 4096
  43.8 1.6 %copy.15 = f32[16,8,256]{2,1,0:T(8,128)} copy(f32[16,8,256]{2,1,0:T(8,128)} %get-tuple-element.8) | data formatting | bytes 262144
Async XLA Ops:
  41.9 1.3 %copy-start = (f32[16,32]{1,0:T(8,128)S(1)}, f32[16,32]{1,0:T(8,128)}, u32[]{:S(2)}) copy-start(f32[16,32]{1,0:T(8,128)} %get-tuple-element.7) | copy-start | bytes 6148
